TPU v7x, 256 devices: a whole 4x4x8 slice. The times are simulated.
256 devices in a mesh: diag: 32 (over x, z_hi, core), off: 8 (over y, z_lo).
Axes of the slice: x: 4, y: 4, z: 8 (z_hi: 4, z_lo: 2; z = z_hi * 2 + z_lo), core: 2. Of those that a mesh axis runs over, the one named last changes fastest.
Arguments:
- bin_embed: bfloat16 [32, 4096], P(None, 'diag'), may hold values from -4.1875 to 4.1875
- weights: bfloat16 [2, 9, 32, 32], replicated, may hold values from -0.375 to 0.375
- biases: float32 [2, 32], replicated, may hold values from -1.8 to 1.8
- dilations: int32 [2], replicated, may hold values from 1 to 8, as said below
- cotangent: bfloat16 [32, 4096, 1024], P(None, 'diag', 'off'), may hold values from -0.29882812 to 0.29882812
Outputs:
- section_out: bfloat16 [32, 4096, 1024], P(None, 'diag', 'off')
- grad_weights: float32 [2, 9, 32, 32], replicated
- grad_biases: float32 [2, 32], replicated
- grad_embed: float32 [32, 4096], P(None, 'diag')
Inputs may be any that keep to these rules, and one draw needn't show every extreme that they name: `dilations`: some layer has dilation exactly 8.
All inputs are finite; a program needn't handle non-finite values.
Results may differ from a plain program's by a relative error of at most 0.0055.
The roundings to bfloat16 on the way count: a program that leaves them out, or rounds other values in their place, can miss the bound.
Values may be sent and summed in bfloat16 or wider, within the bound.
A program may use at most 256 MiB of HBM per device.

v0:
```python
import jax
import jax.numpy as jnp
from jax import lax
from jax.sharding import PartitionSpec as P

DMAX = 8
LAYERS = 2


def extended(array, sides, width):
    for axis, dim in sides:
        size, length = (lax.axis_size(axis), array.shape[dim])
        up = [(i, (i + 1) % size) for i in range(size - 1)]
        down = [(j, i) for i, j in up]
        last = lax.slice_in_dim(array, length - width, length, axis=dim)
        first = lax.slice_in_dim(array, 0, width, axis=dim)
        before = lax.ppermute(last, axis, up)
        after = lax.ppermute(first, axis, down)
        array = jnp.concatenate([before, array, after], axis=dim)
    return array


def from_behind(block, axis, distance):
    devices = range(lax.axis_size(axis))
    route = [(i - distance, i) for i in devices if i - distance in devices]
    return lax.ppermute(block, axis, route)


def band_mask(first_row, first_band, row_count, band_count, total_rows, total_band):
    row_index = first_row + lax.broadcasted_iota(jnp.int32, (row_count, band_count), 0)
    band_index = first_band + lax.broadcasted_iota(jnp.int32, (row_count, band_count), 1)
    inside = (
        (row_index >= 0) & (row_index < total_rows) & (band_index >= 0) & (band_index < total_band)
    )
    return inside & (row_index + band_index < total_rows)


def skew_rows(vector, row_count, band_count):
    length_all = row_count + band_count - 1
    repeated = jnp.tile(vector, (1, row_count + 1))
    flat_view = repeated[:, : row_count * (length_all + 1)]
    return flat_view.reshape(vector.shape[0], row_count, length_all + 1)[:, :, :band_count]


def unskew_sum(pair_grid):
    channels, row_count, band_count = pair_grid.shape
    length_all = row_count + band_count - 1
    padded = jnp.pad(pair_grid, ((0, 0), (0, 0), (0, length_all + 1 - band_count)))
    flat_view = padded.reshape(channels, row_count * (length_all + 1))[:, : row_count * length_all]
    return jnp.sum(flat_view.reshape(channels, row_count, length_all), axis=1, dtype=jnp.float32)


def tap_start(offset_index, direction, dilation):
    vertical = offset_index // 3 - 1
    lateral = offset_index % 3 - 1
    start_row = DMAX + direction * vertical * dilation
    start_band = 2 * DMAX + direction * (lateral - vertical) * dilation
    return (start_row, start_band)


def row_taps(source, kernel_row, direction, dilation, row_count, band_count):
    channels = source.shape[0]
    anchor = jnp.zeros((), jnp.int32)
    pieces = []
    for lateral_index in range(3):
        start_row, start_band = tap_start(3 * kernel_row + lateral_index, direction, dilation)
        pieces.append(
            lax.dynamic_slice(
                source, (anchor, start_row, start_band), (channels, row_count, band_count)
            )
        )
    return jnp.concatenate(pieces, axis=0)


def tap_sum(source, matrices, dilation, direction):
    row_count = source.shape[1] - 2 * DMAX
    band_count = source.shape[2] - 4 * DMAX
    summed = jnp.zeros((matrices.shape[1], row_count, band_count), jnp.float32)
    for kernel_row in range(3):
        stacked = row_taps(source, kernel_row, direction, dilation, row_count, band_count)
        joined = jnp.concatenate(
            [matrices[3 * kernel_row + lateral_index] for lateral_index in range(3)], axis=1
        )
        summed = summed + jnp.einsum(
            "oc,chw->ohw", joined, stacked, preferred_element_type=jnp.float32
        )
    return summed


def tap_grads(grad_pre, relu_rim, dilation):
    channels, row_count, band_count = grad_pre.shape
    tap_terms = []
    for kernel_row in range(3):
        stacked = row_taps(relu_rim, kernel_row, 1, dilation, row_count, band_count)
        joined = jnp.einsum("ohw,chw->oc", grad_pre, stacked, preferred_element_type=jnp.float32)
        for lateral_index in range(3):
            tap_terms.append(joined[:, lateral_index * channels : (lateral_index + 1) * channels])
    return jnp.stack(tap_terms)


def crop_rim(values, rim_depth):
    rows_cut = rim_depth * DMAX
    band_cut = 2 * rim_depth * DMAX
    return values[:, rows_cut : values.shape[1] - rows_cut, band_cut : values.shape[2] - band_cut]


def add_rim(values):
    taller = extended(values, (("diag", 1),), DMAX)
    return extended(taller, (("off", 2),), 2 * DMAX)


def per_device(bin_embed, weights, biases, dilations, cotangent):
    channels, tile_rows = bin_embed.shape
    tile_band = cotangent.shape[2]
    total_rows = tile_rows * lax.axis_size("diag")
    total_band = tile_band * lax.axis_size("off")
    row_start = lax.axis_index("diag") * tile_rows
    band_start = lax.axis_index("off") * tile_band
    rim_depth = 0
    reach = 3 * rim_depth * DMAX
    behind = -(-reach // tile_rows)
    ahead = (total_band + tile_rows - 2 + reach) // tile_rows
    strips = []
    for offset in range(-behind, ahead + 1):
        if offset == 0:
            strips.append(bin_embed)
        else:
            strips.append(from_behind(bin_embed, "diag", -offset))
    nearby = jnp.concatenate(strips, axis=1)
    local_anchor = row_start - behind * tile_rows

    def region(depth):
        return band_mask(
            row_start - depth * DMAX,
            band_start - 2 * depth * DMAX,
            tile_rows + 2 * depth * DMAX,
            tile_band + 4 * depth * DMAX,
            total_rows,
            total_band,
        )

    row_count = tile_rows + 2 * rim_depth * DMAX
    band_count = tile_band + 4 * rim_depth * DMAX
    first_row = row_start - rim_depth * DMAX
    first_band = band_start - 2 * rim_depth * DMAX
    row_part = lax.dynamic_slice_in_dim(nearby, first_row - local_anchor, row_count, 1).astype(
        jnp.float32
    )
    column_slab = lax.dynamic_slice_in_dim(
        nearby, first_row + first_band - local_anchor, row_count + band_count - 1, 1
    )
    column_part = skew_rows(column_slab, row_count, band_count).astype(jnp.float32)
    current_map = jnp.where(region(rim_depth), row_part[:, :, None] + column_part, 0.0).astype(
        jnp.bfloat16
    )
    saved_maps = []
    for layer_index in range(LAYERS):
        current_map = add_rim(current_map)
        rim_depth = 1
        dilation = dilations[layer_index]
        saved_maps.append(crop_rim(current_map, rim_depth - 1))
        conv_out = tap_sum(jnp.maximum(current_map, 0), weights[layer_index], dilation, 1)
        interior = crop_rim(current_map, 1).astype(jnp.float32)
        rim_depth = rim_depth - 1
        updated = interior + conv_out + biases[layer_index][:, None, None]
        current_map = jnp.where(region(rim_depth), updated, 0.0).astype(jnp.bfloat16)
    tile_inside = region(0)
    upstream = cotangent
    weight_grads = [None] * LAYERS
    bias_grads = [None] * LAYERS
    for layer_index in reversed(range(LAYERS)):
        dilation = dilations[layer_index]
        grad_pre = jnp.where(tile_inside, upstream, jnp.zeros((), jnp.bfloat16))
        stored = saved_maps[layer_index]
        weight_grads[layer_index] = tap_grads(grad_pre, jnp.maximum(stored, 0), dilation)
        bias_grads[layer_index] = jnp.sum(grad_pre, axis=(1, 2), dtype=jnp.float32)
        backward = tap_sum(
            add_rim(grad_pre), jnp.transpose(weights[layer_index], (0, 2, 1)), dilation, -1
        )
        gated = jnp.where(crop_rim(stored, 1) > 0, backward, 0.0)
        upstream = (grad_pre.astype(jnp.float32) + gated).astype(jnp.bfloat16)
    grad_pair = jnp.where(tile_inside, upstream, jnp.zeros((), jnp.bfloat16))
    row_part = jnp.sum(grad_pair, axis=2, dtype=jnp.float32)
    column_part = unskew_sum(grad_pair)
    hops = (total_band + tile_rows - 2) // tile_rows
    window = jnp.zeros((channels, (hops + 1) * tile_rows), jnp.float32)
    window = lax.dynamic_update_slice_in_dim(window, column_part, band_start, 1)
    window = window.at[:, :tile_rows].add(row_part)
    band_summed = lax.psum(window, "off")
    grad_embed = band_summed[:, :tile_rows]
    for offset in range(1, hops + 1):
        block_terms = band_summed[:, offset * tile_rows : (offset + 1) * tile_rows]
        grad_embed = grad_embed + from_behind(block_terms, "diag", offset)
    weight_total, bias_total = lax.psum(
        (jnp.stack(weight_grads), jnp.stack(bias_grads)), ("diag", "off")
    )
    return (current_map, weight_total, bias_total, grad_embed)


def solution(mesh):
    placed = (P(None, "diag"), P(), P(), P(), P(None, "diag", "off"))
    return jax.shard_map(
        per_device,
        mesh=mesh,
        in_specs=placed,
        out_specs=(P(None, "diag", "off"), P(), P(), P(None, "diag")),
        check_vma=False,
    )
```

profile of v0, /device:TPU:1, one launch (start us, length us, event | category | flops | bytes accessed | tf_op | source)
XLA Modules:
  0.0 668.4 jit_solution(6654639208555946970)
XLA Ops:
  7.2 5.2 collective-permute-start
  39.7 7.3 %collective-permute-done.5 = bf16[32,128]{1,0:T(8,128)(2,1)S(1)} collective-permute-done((bf16[32,128]{1,0:T(8,128)(2,1)}, bf16[32,128]{1,0:T(8,128)(2,1)S(1)}, u32[]{:S(2)}, u32[]{:S(2)}) %collective-permute-start.5) | collective-permute-done | bytes 8224 | tf_op jit(solution)/shard_map/ppermute | solution.py:26
  47.0 3.2 collective-permute-done.6
  50.3 1.8 collective-permute-done.7
  52.3 3.2 tile.10
  58.4 5.8 convert_reduce_fusion.1
  64.2 5.4 collective-permute-start.16
  69.7 1.9 collective-permute-start.17
  71.6 4.5 collective-permute-start.8
  76.2 1.9 collective-permute-start.9
  81.1 3.3 copy.57
  84.3 3.1 collective-permute-start.18
  87.5 2.1 copy.58
  91.6 2.1 copy.47
  93.8 4.9 collective-permute-start.10
  98.7 2.1 copy.48
  102.1 3.4 copy.59
  105.6 3.5 copy.60
  109.1 3.4 pad_maximum_fusion.6
  112.4 6.0 constant_dynamic-slice_fusion.12
  118.5 3.6 fusion.6
  122.1 2.6 copy.49
  124.7 3.9 fusion
  128.6 3.5 copy.50
  132.1 3.4 maximum_maximum_fusion
  135.5 3.3 constant_dynamic-slice_fusion.26
  140.4 10.8 %select_convert_fusion.1 = bf16[32,128,128]{2,0,1:T(8,128)(2,1)S(1)} fusion(f32[32,128,128]{2,0,1:T(8,128)S(1)} %fusion.51, f32[32,128,128]{2,0,1:T(8,128)S(1)} %fusion.49, bf16[32,128,128]{2,0,1:T(8,128)(2,1)S(1)} %copy-done.1, bf16[32,128,128]{2,0,1:T(8,128)(2,1)S(1)} %get-tuple-element.60, bf16[32,128,128]{2,0,1:T(8,128)(2,1)S(1)} %get-tuple-element.61, ...), kind=kOutput, calls=%fused_computation.54 | convolution fusion | flops 113788928 | bytes 9459840 | tf_op jit(solution)/shard_map/oc,chw->ohw/dot_general | solution.py:84
  156.9 5.4 collective-permute-start.20
  162.3 1.9 collective-permute-start.21
  164.7 4.5 collective-permute-start.12
  169.2 1.9 collective-permute-start.13
  171.7 90.8 %psum.22 = f32[2,32]{1,0:T(2,128)} all-reduce(f32[2,32]{1,0:T(2,128)} %pad_maximum_fusion.37), channel_id=1, replica_groups=mesh['diag'=32,'off'=8] {'diag','off'}, use_global_device_ids=true, to_apply=%region_3.4 | all-reduce | flops 64 | bytes 512 | tf_op jit(solution)/shard_map/psum | solution.py:194
  262.7 2.0 fusion.139
  264.7 3.3 copy.62
  268.0 4.4 collective-permute-start.22
  272.4 3.3 copy.63
  277.6 2.1 copy.51
  279.8 4.7 collective-permute-start.14
  284.5 2.1 copy.52
  287.9 3.5 copy.64
  291.4 3.5 copy.65
  294.9 3.7 pad_maximum_fusion.7
  298.6 6.0 constant_dynamic-slice_fusion.4
  304.7 2.7 fusion.24
  310.0 1.6 convert_reduce_fusion.2
  313.5 2.3 slice_convert_fusion
  315.9 9.5 %reshape.148 = f32[32,128,255]{2,1,0:T(8,128)} reshape(f32[32,32640]{1,0:T(8,128)} %slice_convert_fusion) | data formatting | bytes 8355840 | tf_op jit(solution)/shard_map/convert_element_type | solution.py:50
  325.3 2.6 reduce_sum.38
  331.0 2.6 copy.53
  333.6 3.5 copy.54
  337.1 3.4 maximum_maximum_fusion.1
  340.4 3.3 constant_dynamic-slice_fusion.18
  350.0 4.0 fusion.44
  353.9 49.8 %all-reduce.6.cloned.1.call-done = f32[32,1152]{0,1:T(8,128)} async-done(((f32[32,1152]{0,1:T(8,128)}), f32[32,1152]{0,1:T(8,128)}) %all-reduce.6.cloned.1.call-update) | async-done | bytes 147472 | tf_op jit(solution)/shard_map/psum | solution.py:189
  404.8 9.4 %collective-permute-start.24 = (f32[32,128]{0,1:T(8,128)S(1)}, f32[32,128]{0,1:T(8,128)S(1)}, u32[]{:S(2)}, u32[]{:S(2)}) collective-permute-start(f32[32,128]{0,1:T(8,128)S(1)} %get-tuple-element.84), channel_id=1, source_target_pairs={{0,8},{8,16},{16,24},{24,32},{32,40},{40,48},{48,56},{56,64},{64,7... | collective-permute-start | bytes 49160 | tf_op jit(solution)/shard_map/ppermute | solution.py:26
  414.2 4.5 collective-permute-start.25
  418.7 2.4 collective-permute-start.26
  421.2 2.3 fusion.46
  423.5 5.4 collective-permute-start.27
  428.9 4.7 collective-permute-start.28
  433.6 3.6 collective-permute-start.29
  437.3 5.6 collective-permute-start.30
  448.4 211.0 %all-reduce.4.cloned.1.call-done = f32[2,9,32,32]{3,2,1,0:T(8,128)} async-done(((f32[2,9,32,32]{3,2,1,0:T(8,128)}), f32[2,9,32,32]{3,2,1,0:T(8,128)}) %all-reduce.4.cloned.1.call-update) | async-done | bytes 73744 | tf_op jit(solution)/shard_map/psum | solution.py:194
  659.4 1.7 copy.107
  (263 shorter events, 59.0 us)
Async XLA Ops:
  7.2 396.5 %all-reduce.6.cloned.1.call-start = ((), (), s32[]{:S(2)}) async-start(), calls=%async_computation.1 | async-start | bytes 1179648 | tf_op jit(solution)/shard_map/psum | solution.py:189
  7.2 28.5 %collective-permute-start = (bf16[32,128]{1,0:T(8,128)(2,1)}, bf16[32,128]{1,0:T(8,128)(2,1)S(1)}, u32[]{:S(2)}, u32[]{:S(2)}) collective-permute-start(bf16[32,128]{1,0:T(8,128)(2,1)} %param.7), channel_id=1, source_target_pairs={{8,0},{16,8},{24,16},{32,24},{40,32},{48,40},{56,48},{64,56},{72,6... | collective-permute-start | bytes 24584 | tf_op jit(solution)/shard_map/ppermute | solution.py:26
  12.4 24.6 %collective-permute-start.1 = (bf16[32,128]{1,0:T(8,128)(2,1)}, bf16[32,128]{1,0:T(8,128)(2,1)S(1)}, u32[]{:S(2)}, u32[]{:S(2)}) collective-permute-start(bf16[32,128]{1,0:T(8,128)(2,1)} %param.7), channel_id=1, source_target_pairs={{16,0},{24,8},{32,16},{40,24},{48,32},{56,40},{64,48},{72,56},{80,... | collective-permute-start | bytes 24584 | tf_op jit(solution)/shard_map/ppermute | solution.py:26
  13.7 24.7 %collective-permute-start.2 = (bf16[32,128]{1,0:T(8,128)(2,1)}, bf16[32,128]{1,0:T(8,128)(2,1)S(1)}, u32[]{:S(2)}, u32[]{:S(2)}) collective-permute-start(bf16[32,128]{1,0:T(8,128)(2,1)} %param.7), channel_id=1, source_target_pairs={{24,0},{32,8},{40,16},{48,24},{56,32},{64,40},{72,48},{80,56},{88,... | collective-permute-start | bytes 24584 | tf_op jit(solution)/shard_map/ppermute | solution.py:26
  15.0 24.7 %collective-permute-start.3 = (bf16[32,128]{1,0:T(8,128)(2,1)}, bf16[32,128]{1,0:T(8,128)(2,1)S(1)}, u32[]{:S(2)}, u32[]{:S(2)}) collective-permute-start(bf16[32,128]{1,0:T(8,128)(2,1)} %param.7), channel_id=1, source_target_pairs={{32,0},{40,8},{48,16},{56,24},{64,32},{72,40},{80,48},{88,56},{96,... | collective-permute-start | bytes 24584 | tf_op jit(solution)/shard_map/ppermute | solution.py:26
  16.3 23.4 %collective-permute-start.4 = (bf16[32,128]{1,0:T(8,128)(2,1)}, bf16[32,128]{1,0:T(8,128)(2,1)S(1)}, u32[]{:S(2)}, u32[]{:S(2)}) collective-permute-start(bf16[32,128]{1,0:T(8,128)(2,1)} %param.7), channel_id=1, source_target_pairs={{40,0},{48,8},{56,16},{64,24},{72,32},{80,40},{88,48},{96,56},{104... | collective-permute-start | bytes 24584 | tf_op jit(solution)/shard_map/ppermute | solution.py:26
  35.7 11.3 %collective-permute-start.5 = (bf16[32,128]{1,0:T(8,128)(2,1)}, bf16[32,128]{1,0:T(8,128)(2,1)S(1)}, u32[]{:S(2)}, u32[]{:S(2)}) collective-permute-start(bf16[32,128]{1,0:T(8,128)(2,1)} %param.7), channel_id=1, source_target_pairs={{48,0},{56,8},{64,16},{72,24},{80,32},{88,40},{96,48},{104,56},{11... | collective-permute-start | bytes 24584 | tf_op jit(solution)/shard_map/ppermute | solution.py:26
  37.0 13.2 %collective-permute-start.6 = (bf16[32,128]{1,0:T(8,128)(2,1)}, bf16[32,128]{1,0:T(8,128)(2,1)S(1)}, u32[]{:S(2)}, u32[]{:S(2)}) collective-permute-start(bf16[32,128]{1,0:T(8,128)(2,1)} %param.7), channel_id=1, source_target_pairs={{56,0},{64,8},{72,16},{80,24},{88,32},{96,40},{104,48},{112,56},{1... | collective-permute-start | bytes 24584 | tf_op jit(solution)/shard_map/ppermute | solution.py:26
  38.3 13.7 %collective-permute-start.7 = (bf16[32,128]{1,0:T(8,128)(2,1)}, bf16[32,128]{1,0:T(8,128)(2,1)S(1)}, u32[]{:S(2)}, u32[]{:S(2)}) collective-permute-start(bf16[32,128]{1,0:T(8,128)(2,1)} %param.7), channel_id=1, source_target_pairs={{64,0},{72,8},{80,16},{88,24},{96,32},{104,40},{112,48},{120,56},{... | collective-permute-start | bytes 24584 | tf_op jit(solution)/shard_map/ppermute | solution.py:26
  64.2 26.7 %copy-start = (bf16[32,128,128]{2,0,1:T(8,128)(2,1)}, bf16[32,128,128]{2,0,1:T(8,128)(2,1)S(1)}, u32[]{:S(2)}) copy-start(bf16[32,128,128]{2,0,1:T(8,128)(2,1)S(1)} %get-tuple-element.130) | copy-start | bytes 3145732
  64.2 13.9 %collective-permute-start.16 = (bf16[32,8,128]{2,0,1:T(8,128)(2,1)S(1)}, bf16[32,8,128]{2,0,1:T(8,128)(2,1)S(1)}, u32[]{:S(2)}, u32[]{:S(2)}) collective-permute-start(bf16[32,8,128]{2,0,1:T(8,128)(2,1)S(1)} %get-tuple-element.78), channel_id=1, source_target_pairs={{0,8},{8,16},{16,24},{24,32},{32,40},{40,48},{48,56},{56,64},{64,7... | collective-permute-start | bytes 196616 | tf_op jit(solution)/shard_map/ppermute | solution.py:17
  69.7 8.4 %collective-permute-start.17 = (bf16[32,8,128]{2,0,1:T(8,128)(2,1)S(1)}, bf16[32,8,128]{2,0,1:T(8,128)(2,1)S(1)}, u32[]{:S(2)}, u32[]{:S(2)}) collective-permute-start(bf16[32,8,128]{2,0,1:T(8,128)(2,1)S(1)} %get-tuple-element.79), channel_id=1, source_target_pairs={{8,0},{16,8},{24,16},{32,24},{40,32},{48,40},{56,48},{64,56},{72,6... | collective-permute-start | bytes 196616 | tf_op jit(solution)/shard_map/ppermute | solution.py:18
  71.6 19.3 %collective-permute-start.8 = (bf16[32,8,128]{2,0,1:T(8,128)(2,1)S(1)}, bf16[32,8,128]{2,0,1:T(8,128)(2,1)S(1)}, u32[]{:S(2)}, u32[]{:S(2)}) collective-permute-start(bf16[32,8,128]{2,0,1:T(8,128)(2,1)S(1)} %get-tuple-element.82), channel_id=1, source_target_pairs={{0,8},{8,16},{16,24},{24,32},{32,40},{40,48},{48,56},{56,64},{64,7... | collective-permute-start | bytes 196616 | tf_op jit(solution)/shard_map/ppermute | solution.py:17
  76.2 14.7 %collective-permute-start.9 = (bf16[32,8,128]{2,0,1:T(8,128)(2,1)S(1)}, bf16[32,8,128]{2,0,1:T(8,128)(2,1)S(1)}, u32[]{:S(2)}, u32[]{:S(2)}) collective-permute-start(bf16[32,8,128]{2,0,1:T(8,128)(2,1)S(1)} %get-tuple-element.83), channel_id=1, source_target_pairs={{8,0},{16,8},{24,16},{32,24},{40,32},{48,40},{56,48},{64,56},{72,6... | collective-permute-start | bytes 196616 | tf_op jit(solution)/shard_map/ppermute | solution.py:18
  84.3 17.8 %collective-permute-start.18 = (bf16[32,144,16]{1,2,0:T(8,128)(2,1)}, bf16[32,144,16]{1,2,0:T(8,128)(2,1)}, u32[]{:S(2)}, u32[]{:S(2)}) collective-permute-start(bf16[32,144,16]{1,2,0:T(8,128)(2,1)} %copy.57), channel_id=1, source_target_pairs={{0,1},{1,2},{2,3},{3,4},{4,5},{5,6},{6,7},{8,9},{9,10},{10,11},{11... | collective-permute-start | bytes 442376 | tf_op jit(solution)/shard_map/ppermute | solution.py:17
  89.6 16.0 %collective-permute-start.19 = (bf16[32,144,16]{1,2,0:T(8,128)(2,1)}, bf16[32,144,16]{1,2,0:T(8,128)(2,1)}, u32[]{:S(2)}, u32[]{:S(2)}) collective-permute-start(bf16[32,144,16]{1,2,0:T(8,128)(2,1)} %copy.58), channel_id=1, source_target_pairs={{1,0},{2,1},{3,2},{4,3},{5,4},{6,5},{7,6},{9,8},{10,9},{11,10},{12... | collective-permute-start | bytes 442376 | tf_op jit(solution)/shard_map/ppermute | solution.py:18
  93.8 28.3 %collective-permute-start.10 = (bf16[32,144,16]{1,2,0:T(8,128)(2,1)}, bf16[32,144,16]{1,2,0:T(8,128)(2,1)}, u32[]{:S(2)}, u32[]{:S(2)}) collective-permute-start(bf16[32,144,16]{1,2,0:T(8,128)(2,1)} %copy.47), channel_id=1, source_target_pairs={{0,1},{1,2},{2,3},{3,4},{4,5},{5,6},{6,7},{8,9},{9,10},{10,11},{11... | collective-permute-start | bytes 442376 | tf_op jit(solution)/shard_map/ppermute | solution.py:17
  100.8 27.8 %collective-permute-start.11 = (bf16[32,144,16]{1,2,0:T(8,128)(2,1)}, bf16[32,144,16]{1,2,0:T(8,128)(2,1)}, u32[]{:S(2)}, u32[]{:S(2)}) collective-permute-start(bf16[32,144,16]{1,2,0:T(8,128)(2,1)} %copy.48), channel_id=1, source_target_pairs={{1,0},{2,1},{3,2},{4,3},{5,4},{6,5},{7,6},{9,8},{10,9},{11,10},{12... | collective-permute-start | bytes 442376 | tf_op jit(solution)/shard_map/ppermute | solution.py:18
  118.5 6.2 copy-start.59
  118.5 6.2 copy-start.60
  118.5 6.2 copy-start.61
  124.7 7.4 %copy-start.1 = (bf16[32,128,128]{2,0,1:T(8,128)(2,1)S(1)}, bf16[32,128,128]{2,0,1:T(8,128)(2,1)}, u32[]{:S(2)}) copy-start(bf16[32,128,128]{2,0,1:T(8,128)(2,1)} %copy-done) | copy-start | bytes 3145732
  135.5 3.3 copy-start.53
  135.5 3.3 copy-start.54
  140.3 10.9 %copy-start.17 = (bf16[32,128,128]{2,0,1:T(8,128)(2,1)S(1)}, bf16[32,128,128]{2,0,1:T(8,128)(2,1)}, u32[]{:S(2)}) copy-start(bf16[32,128,128]{2,0,1:T(8,128)(2,1)} %get-tuple-element.43) | copy-start | bytes 3145732
  140.3 10.9 %copy-start.18 = (bf16[32,128,128]{2,0,1:T(8,128)(2,1)S(1)}, bf16[32,128,128]{2,0,1:T(8,128)(2,1)}, u32[]{:S(2)}) copy-start(bf16[32,128,128]{2,0,1:T(8,128)(2,1)} %get-tuple-element.44) | copy-start | bytes 3145732
  140.3 10.9 %copy-start.19 = (bf16[32,128,128]{2,0,1:T(8,128)(2,1)S(1)}, bf16[32,128,128]{2,0,1:T(8,128)(2,1)}, u32[]{:S(2)}) copy-start(bf16[32,128,128]{2,0,1:T(8,128)(2,1)} %get-tuple-element.45) | copy-start | bytes 3145732
  140.3 10.9 %copy-start.56 = (bf16[32,32]{1,0:T(8,128)(2,1)S(1)}, bf16[32,32]{1,0:T(8,128)(2,1)}, u32[]{:S(2)}) copy-start(bf16[32,32]{1,0:T(8,128)(2,1)} %get-tuple-element.121) | copy-start | bytes 6148
  140.3 10.9 %copy-start.57 = (bf16[32,32]{1,0:T(8,128)(2,1)S(1)}, bf16[32,32]{1,0:T(8,128)(2,1)}, u32[]{:S(2)}) copy-start(bf16[32,32]{1,0:T(8,128)(2,1)} %get-tuple-element.122) | copy-start | bytes 6148
  140.3 10.9 %copy-start.58 = (bf16[32,32]{1,0:T(8,128)(2,1)S(1)}, bf16[32,32]{1,0:T(8,128)(2,1)}, u32[]{:S(2)}) copy-start(bf16[32,32]{1,0:T(8,128)(2,1)} %get-tuple-element.123) | copy-start | bytes 6148
  140.3 10.9 %copy-start.66 = (f32[32,128,128]{2,0,1:T(8,128)S(1)}, f32[32,128,128]{2,0,1:T(8,128)}, u32[]{:S(2)}) copy-start(f32[32,128,128]{2,0,1:T(8,128)} %fusion.6) | copy-start | bytes 6291460
  140.3 10.9 %copy-start.67 = (f32[32,128,128]{2,0,1:T(8,128)S(1)}, f32[32,128,128]{2,0,1:T(8,128)}, u32[]{:S(2)}) copy-start(f32[32,128,128]{2,0,1:T(8,128)} %fusion) | copy-start | bytes 6291460
  151.1 125.8 %copy-start.3 = (bf16[32,128,128]{2,0,1:T(8,128)(2,1)}, bf16[32,128,128]{2,0,1:T(8,128)(2,1)S(1)}, u32[]{:S(2)}) copy-start(bf16[32,128,128]{2,0,1:T(8,128)(2,1)S(1)} %select_convert_fusion.1) | copy-start | bytes 3145732
  152.6 109.9 %copy-start.5 = (bf16[32,128,128]{2,0,1:T(8,128)(2,1)}, bf16[32,128,128]{2,0,1:T(8,128)(2,1)S(1)}, u32[]{:S(2)}) copy-start(bf16[32,128,128]{2,0,1:T(8,128)(2,1)S(1)} %get-tuple-element.136) | copy-start | bytes 3145732
  155.7 15.5 %copy-start.62 = (f32[32]{0:T(128)S(1)}, f32[32]{0:T(128)}, u32[]{:S(2)}) copy-start(f32[32]{0:T(128)} %get-tuple-element.32) | copy-start | bytes 388
  156.9 105.7 %collective-permute-start.20 = (bf16[32,8,128]{2,0,1:T(8,128)(2,1)}, bf16[32,8,128]{2,0,1:T(8,128)(2,1)S(1)}, u32[]{:S(2)}, u32[]{:S(2)}) collective-permute-start(bf16[32,8,128]{2,0,1:T(8,128)(2,1)} %get-tuple-element.76), channel_id=1, source_target_pairs={{0,8},{8,16},{16,24},{24,32},{32,40},{40,48},{48,56},{56,64},{64,7... | collective-permute-start | bytes 196616 | tf_op jit(solution)/shard_map/ppermute | solution.py:17
  162.3 100.3 %collective-permute-start.21 = (bf16[32,8,128]{2,0,1:T(8,128)(2,1)}, bf16[32,8,128]{2,0,1:T(8,128)(2,1)S(1)}, u32[]{:S(2)}, u32[]{:S(2)}) collective-permute-start(bf16[32,8,128]{2,0,1:T(8,128)(2,1)} %get-tuple-element.77), channel_id=1, source_target_pairs={{8,0},{16,8},{24,16},{32,24},{40,32},{48,40},{56,48},{64,56},{72,6... | collective-permute-start | bytes 196616 | tf_op jit(solution)/shard_map/ppermute | solution.py:18
  164.7 4.6 copy-start.33
  164.7 112.2 %collective-permute-start.12 = (bf16[32,8,128]{2,0,1:T(8,128)(2,1)S(1)}, bf16[32,8,128]{2,0,1:T(8,128)(2,1)S(1)}, u32[]{:S(2)}, u32[]{:S(2)}) collective-permute-start(bf16[32,8,128]{2,0,1:T(8,128)(2,1)S(1)} %get-tuple-element.80), channel_id=1, source_target_pairs={{0,8},{8,16},{16,24},{24,32},{32,40},{40,48},{48,56},{56,64},{64,7... | collective-permute-start | bytes 196616 | tf_op jit(solution)/shard_map/ppermute | solution.py:17
  169.2 107.7 %collective-permute-start.13 = (bf16[32,8,128]{2,0,1:T(8,128)(2,1)S(1)}, bf16[32,8,128]{2,0,1:T(8,128)(2,1)S(1)}, u32[]{:S(2)}, u32[]{:S(2)}) collective-permute-start(bf16[32,8,128]{2,0,1:T(8,128)(2,1)S(1)} %get-tuple-element.81), channel_id=1, source_target_pairs={{8,0},{16,8},{24,16},{32,24},{40,32},{48,40},{56,48},{64,56},{72,6... | collective-permute-start | bytes 196616 | tf_op jit(solution)/shard_map/ppermute | solution.py:18
  268.0 19.9 %collective-permute-start.22 = (bf16[32,144,16]{1,2,0:T(8,128)(2,1)}, bf16[32,144,16]{1,2,0:T(8,128)(2,1)}, u32[]{:S(2)}, u32[]{:S(2)}) collective-permute-start(bf16[32,144,16]{1,2,0:T(8,128)(2,1)} %copy.62), channel_id=1, source_target_pairs={{0,1},{1,2},{2,3},{3,4},{4,5},{5,6},{6,7},{8,9},{9,10},{10,11},{11... | collective-permute-start | bytes 442376 | tf_op jit(solution)/shard_map/ppermute | solution.py:17
  275.6 15.7 %collective-permute-start.23 = (bf16[32,144,16]{1,2,0:T(8,128)(2,1)}, bf16[32,144,16]{1,2,0:T(8,128)(2,1)}, u32[]{:S(2)}, u32[]{:S(2)}) collective-permute-start(bf16[32,144,16]{1,2,0:T(8,128)(2,1)} %copy.63), channel_id=1, source_target_pairs={{1,0},{2,1},{3,2},{4,3},{5,4},{6,5},{7,6},{9,8},{10,9},{11,10},{12... | collective-permute-start | bytes 442376 | tf_op jit(solution)/shard_map/ppermute | solution.py:18
  279.8 51.2 %collective-permute-start.14 = (bf16[32,144,16]{1,2,0:T(8,128)(2,1)}, bf16[32,144,16]{1,2,0:T(8,128)(2,1)}, u32[]{:S(2)}, u32[]{:S(2)}) collective-permute-start(bf16[32,144,16]{1,2,0:T(8,128)(2,1)} %copy.51), channel_id=1, source_target_pairs={{0,1},{1,2},{2,3},{3,4},{4,5},{5,6},{6,7},{8,9},{9,10},{10,11},{11... | collective-permute-start | bytes 442376 | tf_op jit(solution)/shard_map/ppermute | solution.py:17
  286.6 47.0 %collective-permute-start.15 = (bf16[32,144,16]{1,2,0:T(8,128)(2,1)}, bf16[32,144,16]{1,2,0:T(8,128)(2,1)}, u32[]{:S(2)}, u32[]{:S(2)}) collective-permute-start(bf16[32,144,16]{1,2,0:T(8,128)(2,1)} %copy.52), channel_id=1, source_target_pairs={{1,0},{2,1},{3,2},{4,3},{5,4},{6,5},{7,6},{9,8},{10,9},{11,10},{12... | collective-permute-start | bytes 442376 | tf_op jit(solution)/shard_map/ppermute | solution.py:18
  327.9 9.1 %copy-start.4 = (bf16[32,128,128]{2,0,1:T(8,128)(2,1)S(1)}, bf16[32,128,128]{2,0,1:T(8,128)(2,1)}, u32[]{:S(2)}) copy-start(bf16[32,128,128]{2,0,1:T(8,128)(2,1)} %copy-done.3) | copy-start | bytes 3145732
  330.7 328.7 %all-reduce.4.cloned.1.call-start = ((), (), s32[]{:S(2)}) async-start(), calls=%async_computation | async-start | bytes 589824 | tf_op jit(solution)/shard_map/psum | solution.py:194
  343.8 4.0 copy-start.9
  343.8 4.0 copy-start.11
  349.9 71.1 %copy-start.14 = (bf16[32,128,128]{2,0,1:T(8,128)(2,1)S(1)}, bf16[32,128,128]{2,0,1:T(8,128)(2,1)}, u32[]{:S(2)}) copy-start(bf16[32,128,128]{2,0,1:T(8,128)(2,1)} %copy-done.13) | copy-start | bytes 3145732
  404.8 28.8 %collective-permute-start.24 = (f32[32,128]{0,1:T(8,128)S(1)}, f32[32,128]{0,1:T(8,128)S(1)}, u32[]{:S(2)}, u32[]{:S(2)}) collective-permute-start(f32[32,128]{0,1:T(8,128)S(1)} %get-tuple-element.84), channel_id=1, source_target_pairs={{0,8},{8,16},{16,24},{24,32},{32,40},{40,48},{48,56},{56,64},{64,7... | collective-permute-start | bytes 49160 | tf_op jit(solution)/shard_map/ppermute | solution.py:26
  414.2 23.1 %collective-permute-start.25 = (f32[32,128]{0,1:T(8,128)S(1)}, f32[32,128]{0,1:T(8,128)S(1)}, u32[]{:S(2)}, u32[]{:S(2)}) collective-permute-start(f32[32,128]{0,1:T(8,128)S(1)} %get-tuple-element.91), channel_id=1, source_target_pairs={{0,16},{8,24},{16,32},{24,40},{32,48},{40,56},{48,64},{56,72},{64,... | collective-permute-start | bytes 49160 | tf_op jit(solution)/shard_map/ppermute | solution.py:26
  418.7 24.2 %collective-permute-start.26 = (f32[32,128]{0,1:T(8,128)S(1)}, f32[32,128]{0,1:T(8,128)S(1)}, u32[]{:S(2)}, u32[]{:S(2)}) collective-permute-start(f32[32,128]{0,1:T(8,128)S(1)} %get-tuple-element.90), channel_id=1, source_target_pairs={{0,24},{8,32},{16,40},{24,48},{32,56},{40,64},{48,72},{56,80},{64,... | collective-permute-start | bytes 49160 | tf_op jit(solution)/shard_map/ppermute | solution.py:26
  421.1 23.1 %copy-start.10 = (bf16[32,128,128]{2,0,1:T(8,128)(2,1)S(1)}, bf16[32,128,128]{2,0,1:T(8,128)(2,1)}, u32[]{:S(2)}) copy-start(bf16[32,128,128]{2,0,1:T(8,128)(2,1)} %copy-done.9) | copy-start | bytes 3145732
  421.1 23.1 %copy-start.12 = (bf16[32,128,128]{2,0,1:T(8,128)(2,1)S(1)}, bf16[32,128,128]{2,0,1:T(8,128)(2,1)}, u32[]{:S(2)}) copy-start(bf16[32,128,128]{2,0,1:T(8,128)(2,1)} %copy-done.11) | copy-start | bytes 3145732
  421.1 23.1 %copy-start.35 = (bf16[32,32]{1,0:T(8,128)(2,1)S(1)}, bf16[32,32]{1,0:T(8,128)(2,1)}, u32[]{:S(2)}) copy-start(bf16[32,32]{1,0:T(8,128)(2,1)} %get-tuple-element.94) | copy-start | bytes 6148
  421.1 23.1 %copy-start.36 = (bf16[32,32]{1,0:T(8,128)(2,1)S(1)}, bf16[32,32]{1,0:T(8,128)(2,1)}, u32[]{:S(2)}) copy-start(bf16[32,32]{1,0:T(8,128)(2,1)} %get-tuple-element.95) | copy-start | bytes 6148
  421.1 23.1 %copy-start.37 = (bf16[32,32]{1,0:T(8,128)(2,1)S(1)}, bf16[32,32]{1,0:T(8,128)(2,1)}, u32[]{:S(2)}) copy-start(bf16[32,32]{1,0:T(8,128)(2,1)} %get-tuple-element.111) | copy-start | bytes 6148
  421.1 23.1 %copy-start.63 = (f32[32]{0:T(128)S(1)}, f32[32]{0:T(128)}, u32[]{:S(2)}) copy-start(f32[32]{0:T(128)} %get-tuple-element.131) | copy-start | bytes 388
  421.1 23.1 %copy-start.65 = (f32[32,128,128]{2,0,1:T(8,128)S(1)}, f32[32,128,128]{2,0,1:T(8,128)}, u32[]{:S(2)}) copy-start(f32[32,128,128]{2,0,1:T(8,128)} %fusion.44) | copy-start | bytes 6291460
  423.5 23.3 %collective-permute-start.27 = (f32[32,128]{0,1:T(8,128)S(1)}, f32[32,128]{0,1:T(8,128)S(1)}, u32[]{:S(2)}, u32[]{:S(2)}) collective-permute-start(f32[32,128]{0,1:T(8,128)S(1)} %get-tuple-element.89), channel_id=1, source_target_pairs={{0,32},{8,40},{16,48},{24,56},{32,64},{40,72},{48,80},{56,88},{64,... | collective-permute-start | bytes 49160 | tf_op jit(solution)/shard_map/ppermute | solution.py:26
  428.9 17.8 %collective-permute-start.28 = (f32[32,128]{0,1:T(8,128)S(1)}, f32[32,128]{0,1:T(8,128)S(1)}, u32[]{:S(2)}, u32[]{:S(2)}) collective-permute-start(f32[32,128]{0,1:T(8,128)S(1)} %get-tuple-element.88), channel_id=1, source_target_pairs={{0,40},{8,48},{16,56},{24,64},{32,72},{40,80},{48,88},{56,96},{64,... | collective-permute-start | bytes 49160 | tf_op jit(solution)/shard_map/ppermute | solution.py:26
  433.6 13.2 %collective-permute-start.29 = (f32[32,128]{0,1:T(8,128)S(1)}, f32[32,128]{0,1:T(8,128)S(1)}, u32[]{:S(2)}, u32[]{:S(2)}) collective-permute-start(f32[32,128]{0,1:T(8,128)S(1)} %get-tuple-element.87), channel_id=1, source_target_pairs={{0,48},{8,56},{16,64},{24,72},{32,80},{40,88},{48,96},{56,104},{64... | collective-permute-start | bytes 49160 | tf_op jit(solution)/shard_map/ppermute | solution.py:26
  437.3 9.5 %collective-permute-start.30 = (f32[32,128]{0,1:T(8,128)S(1)}, f32[32,128]{0,1:T(8,128)S(1)}, u32[]{:S(2)}, u32[]{:S(2)}) collective-permute-start(f32[32,128]{0,1:T(8,128)S(1)} %get-tuple-element.86), channel_id=1, source_target_pairs={{0,56},{8,64},{16,72},{24,80},{32,88},{40,96},{48,104},{56,112},{6... | collective-permute-start | bytes 49160 | tf_op jit(solution)/shard_map/ppermute | solution.py:26
  442.9 3.9 collective-permute-start.31
  (39 other events, 69.7 us)
Sparse Core Ops, SparseCore 0:
  330.8 72.8 all-reduce.5
  409.8 249.5 all-reduce.3
where the time goes:
time: 679 us; the launch traced here: 668 us
  waiting for transfers between devices  273 us (40%)
  local copies, waits for them, and re-layouts  109 us (16%)
  starting transfers between devices  101 us (15%)
  blocking collectives  90.8 us (13%)
  matrix products  40.1 us (6%)
  other arithmetic  28.9 us (4%)
  between operations  25 us (4%)
    psum x1, waiting for transfers between devices, per_device(): lax.psum((jnp.stack(weight_grads), jnp.stack(bias_grads)), ('diag', 'off'))  211 us
    psum x1, blocking collectives, per_device(): lax.psum((jnp.stack(weight_grads), jnp.stack(bias_grads)), ('diag', 'off'))  90.8 us
    ppermute x16, starting transfers between devices, from_behind(): return lax.ppermute(block, axis, route)  51.1 us
    psum x1, waiting for transfers between devices, per_device(): band_summed = lax.psum(window, 'off')  49.8 us
    ppermute x8, starting transfers between devices, extended(): before = lax.ppermute(last, axis, up)  37 us
    dot_general x12, matrix products, tap_sum(): jnp.einsum('oc,chw->ohw', joined, stacked, preferred_element_type=jnp.flo...  33.1 us
    dynamic_slice x4, local copies, waits for them, and re-layouts, row_taps(): lax.dynamic_slice(source, (anchor, start_row, start_band), (channels, row...  18.7 us
    slice x12, local copies, waits for them, and re-layouts, extended(): last = lax.slice_in_dim(array, length - width, length, axis=dim)  16.2 us
  transfers between devices with their start and end apart: 34, of which 5 were waited for; matrix products, arithmetic and copies ran while one was open for 20% of the time, Pallas kernels for 0%

commit v1 on v0

v1 whole, which is shorter than its diff:
```python
import jax
import jax.numpy as jnp
from jax import lax
from jax.experimental import pallas as pl
from jax.experimental.pallas import tpu as pltpu
from jax.sharding import PartitionSpec as P

DMAX = 8
CH = 32
TI = 128
TK = 128
H1 = TI + 2 * DMAX
H2 = TI + 4 * DMAX
NBINS = 4096
KBAND = 1024
bf16 = jnp.bfloat16
f32 = jnp.float32
NT = (((1,), (1,)), ((), ()))


def lanes(n=1):
    return lax.broadcasted_iota(jnp.int32, (CH, 128), 1)


def in_range(amount):
    p = lanes() + amount
    return (p >= 0) & (p < 128)


def turned(x, amount):
    return pltpu.roll(x, lax.rem(256 - amount, 128), 1)


def shift_pair(a, b, amount, inside, both=True):
    ra, rb = turned(a, amount), turned(b, amount)
    out_a = jnp.where(inside, ra, rb)
    if not both:
        return out_a
    return out_a, jnp.where(inside, rb, ra)


def row_masks(row0, band0, i):
    p = lanes()
    row = row0 + i
    ka = band0 + p
    kb = band0 + jnp.where(p < 64, p + 128, p - 128)
    live = (row >= 0)
    ma = (ka < NBINS - row) & live
    mb = (kb < NBINS - row) & (kb >= 0) & (kb < KBAND) & live
    return ma, mb


def store_shifts(dst, i, a, b, amounts, insides, both=True):
    for n, s in enumerate((-2, -1, 0, 1, 2)):
        rows = slice(CH * n, CH * (n + 1))
        if s == 0:
            dst[i, rows, 0:128] = a
            if both:
                dst[i, rows, 128:256] = b
        elif both:
            sa, sb = shift_pair(a, b, amounts[n], insides[n])
            dst[i, rows, 0:128] = sa
            dst[i, rows, 128:256] = sb
        else:
            dst[i, rows, 0:128] = shift_pair(a, b, amounts[n], insides[n], False)


def taps(src, i, d, lo=0, hi=256):
    return jnp.concatenate(
        [src[i - d, 64:160, lo:hi], src[i, 32:128, lo:hi], src[i + d, 0:96, lo:hi]], axis=0
    )


def shift_tables(d):
    amounts = [s * d for s in (-2, -1, 0, 1, 2)]
    return amounts, [in_range(t) for t in amounts]


def phase_x0(row0, band0, d, ec, er, x0, s0, unroll=4):
    amounts, insides = shift_tables(d)

    def body(it, _):
        for w in range(unroll):
            j = it * unroll + w
            i = j - 2 * DMAX
            q = lax.div(i + 128, 128) - 1
            t = i - q * 128
            back = lax.rem(128 - t, 128)
            re = [pltpu.roll(ec[q + 1 + n], back, 1) for n in range(4)]
            cut = lanes() < 128 - t
            wm = jnp.where(cut, re[0], re[1])
            w0 = jnp.where(cut, re[1], re[2])
            w1 = jnp.where(cut, re[2], re[3])
            wb = jnp.where(lanes() < 64, w1, wm)
            own = pltpu.roll(er[q + 1], back, 1).astype(f32)[:, 0:1]
            ma, mb = row_masks(row0, band0, i)
            a = jnp.where(ma, own + w0.astype(f32), 0.0).astype(bf16)
            b = jnp.where(mb, own + wb.astype(f32), 0.0).astype(bf16)
            x0[j, :, 0:128] = a
            x0[j, :, 128:256] = b
            store_shifts(s0, j, jnp.maximum(a, 0), jnp.maximum(b, 0), amounts, insides)
        return 0

    lax.fori_loop(0, H2 // unroll, body, 0)


def phase_x1(row0, band0, d, dn, wf, bias, x0, s0, x1, s1, unroll=4):
    amounts, insides = shift_tables(dn)
    bias = jnp.broadcast_to(bias, (CH, 128))

    def body(it, _):
        for w in range(unroll):
            j = it * unroll + w
            jj = j + DMAX
            conv = jnp.dot(wf, taps(s0, jj, d), preferred_element_type=f32)
            ma, mb = row_masks(row0, band0, j - DMAX)
            a = x0[jj, :, 0:128].astype(f32) + conv[:, 0:128] + bias
            b = x0[jj, :, 128:256].astype(f32) + conv[:, 128:256] + bias
            a = jnp.where(ma, a, 0.0).astype(bf16)
            b = jnp.where(mb, b, 0.0).astype(bf16)
            x1[j, :, 0:128] = a
            x1[j, :, 128:256] = b
            store_shifts(s1, j, jnp.maximum(a, 0), jnp.maximum(b, 0), amounts, insides, False)
        return 0

    lax.fori_loop(0, H1 // unroll, body, 0)


def phase_x2(row0, band0, d, wf, bias, x1, s1, out, unroll=16):
    bias = jnp.broadcast_to(bias, (CH, 128))

    def body(it, _):
        rows = []
        for w in range(0, unroll, 2):
            i = it * unroll + w
            j = i + DMAX
            x = jnp.concatenate([taps(s1, j, d, 0, 128), taps(s1, j + 1, d, 0, 128)], axis=1)
            conv = jnp.dot(wf, x, preferred_element_type=f32)
            for z in range(2):
                ma, _mb = row_masks(row0, band0, i + z)
                a = x1[j + z, :, 0:128].astype(f32) + conv[:, 128 * z : 128 * z + 128] + bias
                rows.append(jnp.where(ma, a, 0.0).astype(bf16))
        out[:, pl.ds(pl.multiple_of(it * unroll, unroll), unroll), :] = jnp.swapaxes(jnp.stack(rows), 0, 1)
        return 0

    lax.fori_loop(0, TI // unroll, body, 0)


def phase_gw(h, hoff, s, soff, d, gw, gb, unroll=4):
    def body(it, carry):
        acc, accb = carry
        for w in range(0, unroll, 2):
            i = it * unroll + w
            x = jnp.concatenate(
                [taps(s, i + soff, d, 0, 128), taps(s, i + 1 + soff, d, 0, 128)], axis=1
            )
            ha = h[i + hoff, 64:96, 0:128]
            hb = h[i + hoff + 1, 64:96, 0:128]
            hh = jnp.concatenate([ha, hb], axis=1)
            acc = acc + lax.dot_general(hh, x, NT, preferred_element_type=f32)
            accb = accb + (ha.astype(f32) + hb.astype(f32))
        return acc, accb

    acc, accb = lax.fori_loop(
        0, TI // unroll, body, (jnp.zeros((CH, 9 * CH), f32), jnp.zeros((CH, 128), f32))
    )
    gw[...] = acc
    gb[...] = accb


def phase_h(row0, band0, d, a_rows, rl, rr, t1):
    amounts, insides = shift_tables(d)

    def body(it, _):
        pl_, pr_ = rl[it], rr[it]
        for w in range(4):
            j = it * 4 + w
            ma, mb = row_masks(row0, band0, j - 2 * DMAX)
            right = pltpu.roll(pl_, (128 - 32 * w) % 128, 1) if w else pl_
            left = pltpu.roll(pr_, 32 * (3 - w), 1) if w < 3 else pr_
            b = jnp.where(lanes() < 64, right, left)
            a = jnp.where(ma, a_rows[j], 0)
            b = jnp.where(mb, b, 0)
            store_shifts(t1, j, a, b, amounts, insides)
        return 0

    lax.fori_loop(0, H2 // 4, body, 0)


def phase_g1(d, dn, wb, x1, t1, t0, unroll=4):
    amounts, insides = shift_tables(dn)

    def body(it, _):
        for w in range(unroll):
            j = it * unroll + w
            jj = j + DMAX
            q = jnp.dot(wb, taps(t1, jj, d), preferred_element_type=f32)
            ab = []
            for z in range(2):
                sl = slice(128 * z, 128 * z + 128)
                h = t1[jj, 64:96, sl].astype(f32)
                gate = x1[j, :, sl].astype(f32) > 0
                ab.append((h + jnp.where(gate, q[:, sl], 0.0)).astype(bf16))
            store_shifts(t0, j, ab[0], ab[1], amounts, insides, False)
        return 0

    lax.fori_loop(0, H1 // unroll, body, 0)


def phase_g0(d, wb, x0, t0, unroll=4):
    lane = lanes()

    def body(it, carry):
        rsum, lo, hi = carry
        for w in range(0, unroll, 2):
            i = it * unroll + w
            j = i + DMAX
            x = jnp.concatenate([taps(t0, j, d, 0, 128), taps(t0, j + 1, d, 0, 128)], axis=1)
            q = jnp.dot(wb, x, preferred_element_type=f32)
            for z in range(2):
                g1 = t0[j + z, 64:96, 0:128].astype(f32)
                gate = x0[j + z + DMAX, :, 0:128].astype(f32) > 0
                gp = (g1 + jnp.where(gate, q[:, 128 * z : 128 * z + 128], 0.0)).astype(bf16)
                gf = gp.astype(f32)
                rsum = jnp.where(lane == i + z, jnp.sum(gf, axis=1, keepdims=True), rsum)
                moved = pltpu.roll(gp, i + z, 1).astype(f32)
                low = jnp.where(lane >= i + z, moved, 0.0)
                lo = lo + low
                hi = hi + (moved - low)
        return rsum, lo, hi

    zero = jnp.zeros((CH, 128), f32)
    return lax.fori_loop(0, TI // unroll, body, (zero, zero, zero))
MESH = pl.DeviceIdType.MESH
NR, NO = 32, 8


def place_weights(w, wf, wb):
    row = lax.broadcasted_iota(jnp.int32, (CH, 9 * CH), 0)
    col = lax.broadcasted_iota(jnp.int32, (CH, 9 * CH), 1)
    for layer in range(2):
        fwd = jnp.zeros((CH, 9 * CH), f32)
        bwd = jnp.zeros((CH, 9 * CH), f32)
        for t in range(9):
            spot = jnp.where(col == row + CH * t, 1.0, 0.0).astype(bf16)
            fwd = fwd + jnp.dot(w[layer, t], spot, preferred_element_type=f32)
            bwd = bwd + lax.dot_general(
                w[layer, 8 - t], spot, (((0,), (0,)), ((), ())), preferred_element_type=f32
            )
        wf[layer] = fwd.astype(bf16)
        wb[layer] = bwd.astype(bf16)


def pack_grads(layer, gw, gb, pay):
    third = jnp.concatenate([gw[:, 256:288], jnp.sum(gb[...], axis=1, keepdims=True), jnp.zeros((CH, 95), f32)], axis=1)
    for og in range(4):
        rows = slice(8 * og, 8 * og + 8)
        for lt in range(2):
            pay[layer * 8 + og * 2 + lt, 0] = gw[rows, 128 * lt : 128 * lt + 128]
    return third


def unpack_grads(res, gw_out, gb_out):
    eye = lax.broadcasted_iota(jnp.int32, (CH, CH), 0) == lax.broadcasted_iota(jnp.int32, (CH, CH), 1)
    third = jnp.concatenate([res[og, 1] for og in range(4)], axis=0)
    for layer in range(2):
        for lt in range(2):
            tile = jnp.concatenate([res[layer * 8 + og * 2 + lt, 0] for og in range(4)], axis=0)
            for n in range(4):
                gw_out[layer, 4 * lt + n] = tile[:, CH * n : CH * n + CH]
        gw_out[layer, 8] = third[:, 64 * layer : 64 * layer + CH]
        column = third[:, 64 * layer + CH : 64 * layer + CH + 1]
        gb_out[layer : layer + 1, :] = jnp.sum(jnp.where(eye, column, 0.0), axis=0, keepdims=True)


def remote(src, dst, send, recv, target):
    return pltpu.make_async_remote_copy(
        src_ref=src, dst_ref=dst, send_sem=send, recv_sem=recv, device_id=target, device_id_type=MESH
    )


def wrap(r, o):
    return (lax.rem(r + 2 * NR, NR), lax.rem(o + NO, NO))


def halo_copies(r, o, a, pl_, pr_, rl, rr, send, recv):
    last, first = slice(112, 128), slice(0, 16)
    jobs = [
        (a.at[16 + 112 : 16 + 128], a.at[0:16], 1, 0),
        (a.at[16:32], a.at[144:160], -1, 0),
        (pl_, rl.at[4:36], 0, -1),
        (pr_, rr.at[4:36], 0, 1),
        (pl_.at[28:32], rl.at[0:4], 1, -1),
        (pl_.at[0:4], rl.at[36:40], -1, -1),
        (pr_.at[28:32], rr.at[0:4], 1, 1),
        (pr_.at[0:4], rr.at[36:40], -1, 1),
    ]
    return [
        remote(src, dst, send.at[n], recv.at[n], wrap(r + dr, o + do))
        for n, (src, dst, dr, do) in enumerate(jobs)
    ]


def embed_copies(r, o, emb, ec, er, send, recv):
    other = o + 1 - 2 * lax.rem(o, 2)
    copies = [
        remote(emb, ec.at[n], send.at[n - 1], recv.at[n - 1], wrap(r - other - (n - 2), other))
        for n in range(1, 5)
    ]
    copies.append(remote(emb, er.at[0], send.at[4], recv.at[4], wrap(r + 1, o)))
    copies.append(remote(emb, er.at[2], send.at[5], recv.at[5], wrap(r - 1, o)))
    return copies


def greet_exchange(r, o, barrier):
    other = o + 1 - 2 * lax.rem(o, 2)
    targets = [wrap(r + o + n - 2, other) for n in range(1, 5)]
    targets += [wrap(r + dr, o + do) for dr in (-1, 0, 1) for do in (-1, 0, 1) if (dr, do) != (0, 0)]
    for target in targets:
        pl.semaphore_signal(barrier, inc=1, device_id=target, device_id_type=MESH)
    return len(targets)


def lay_rows(cot, a, pl_, pr_):
    lane = lanes()

    def body(it, _):
        block = jnp.swapaxes(cot[:, pl.ds(pl.multiple_of(it * 16, 16), 16), :], 0, 1)
        a[pl.ds(16 + it * 16, 16)] = block
        for n in range(4):
            left = block[4 * n]
            right = block[4 * n + 3]
            for w in range(1, 4):
                left = jnp.where(lane < 32 * w, left, pltpu.roll(block[4 * n + w], 32 * w, 1))
            for w in range(2, -1, -1):
                right = jnp.where(lane >= 32 * (w + 1), right, pltpu.roll(block[4 * n + w], 128 - 32 * (3 - w), 1))
            pl_[it * 4 + n] = left
            pr_[it * 4 + n] = right
        return 0

    lax.fori_loop(0, 8, body, 0)


def exchange_kernel(emb, cot, ec, er, a, rl, rr, pl_, pr_, esend, erecv, hsend, hrecv):
    r, o = lax.axis_index("diag"), lax.axis_index("off")
    barrier = pltpu.get_barrier_semaphore()
    count = greet_exchange(r, o, barrier)
    ec[0] = jnp.zeros((CH, 128), bf16)
    ec[5] = jnp.zeros((CH, 128), bf16)
    er[1] = emb[...]
    pl.semaphore_wait(barrier, count)
    ecopies = embed_copies(r, o, emb, ec, er, esend, erecv)
    for c in ecopies:
        c.start()
    lay_rows(cot, a, pl_, pr_)
    hcopies = halo_copies(r, o, a, pl_, pr_, rl, rr, hsend, hrecv)
    for c in hcopies:
        c.start()
    for c in ecopies + hcopies:
        c.wait()


def compute_kernel(
    dil, ec, er, a_rows, rl, rr, w, bias, out, pay, emb, x0, x1, s0, t1, s1, t0, wf, wb, gw, gb
):
    r, o = lax.axis_index("diag"), lax.axis_index("off")
    d0, d1 = dil[0], dil[1]
    row0, band0 = r * TI, o * TK
    place_weights(w, wf, wb)
    eye = lax.broadcasted_iota(jnp.int32, (CH, CH), 0) == lax.broadcasted_iota(jnp.int32, (CH, CH), 1)

    def column(layer):
        return jnp.sum(jnp.where(eye, bias[layer : layer + 1, :], 0.0), axis=1, keepdims=True)

    phase_x0(row0, band0, d0, ec, er, x0, s0, 8)
    phase_x1(row0, band0, d0, d1, wf[0], column(0), x0, s0, x1, s1, 16)
    phase_x2(row0, band0, d1, wf[1], column(1), x1, s1, out, 32)
    phase_h(row0, band0, d1, a_rows, rl, rr, t1)
    phase_gw(t1, 16, s1, 8, d1, gw, gb, 16)
    third1 = pack_grads(1, gw, gb, pay)
    phase_g1(d1, d0, wb[1], x1, t1, t0, 16)
    phase_gw(t0, 8, s0, 16, d0, gw, gb, 16)
    third0 = pack_grads(0, gw, gb, pay)
    third = third0 + pltpu.roll(third1, 64, 1)
    for n in range(16):
        pay[n, 1] = third[8 * n : 8 * n + 8] if n < 4 else jnp.zeros((8, 128), f32)
    rsum, lo, hi = phase_g0(d0, wb[0], x0, t0, 16)
    emb[0] = rsum
    emb[1] = lo
    emb[2] = hi


def reduce_kernel(
    pay, emb, gw_out, gb_out, emb_out, wr1, w2, wr2, res, er, s1, r1, s2, r2, s3, r3, es, erc, ls
):
    r, o = lax.axis_index("diag"), lax.axis_index("off")
    core, b = lax.rem(r, 2), lax.div(r, 2)
    me = o * 2 + core
    barrier = pltpu.get_barrier_semaphore()

    def peer_a(n):
        other = lax.rem(me + n, 16)
        return other, (2 * b + lax.rem(other, 2), lax.div(other, 2))

    def peer_b(n):
        other = lax.rem(b + n, 16)
        return other, (2 * other + core, o)

    def greet(target):
        pl.semaphore_signal(barrier, inc=1, device_id=target, device_id_type=MESH)

    for n in range(1, 16):
        greet(peer_a(n)[1])
        greet(peer_b(n)[1])
    for n in range(1, 8):
        oo = lax.rem(o + n, 8)
        greet(wrap(r, oo))
        greet(wrap(r - oo, oo))
        greet(wrap(r - oo - 1, oo))
    greet(wrap(r - o - 1, o))

    @pl.when(o > 0)
    def _():
        greet(wrap(r - o, o))

    pl.semaphore_wait(barrier, 30 + 21 + 1 + jnp.minimum(o, 1))

    first = [remote(pay.at[other], wr1.at[me], s1.at[n], r1.at[me], target)
             for n in range(1, 16) for other, target in [peer_a(n)]]
    for c in first:
        c.start()
    eout = []
    for n in range(0, 8):
        oo = lax.rem(o + n, 8)
        for kind, dr in ((0, 0), (1, o), (2, o + 1)):
            if n == 0 and kind < 2:
                continue
            eout.append(remote(emb.at[kind], er.at[kind * 8 + o], es.at[kind * 8 + n], erc.at[kind * 8 + o], wrap(r + dr, oo)))
    for c in eout:
        c.start()
    own = remote(emb.at[1], er.at[8 + o], es.at[8], erc.at[8 + o], wrap(r + o, o))

    @pl.when(o > 0)
    def _():
        own.start()

    local = pltpu.make_async_copy(emb.at[1], er.at[8 + o], ls)

    @pl.when(o == 0)
    def _():
        local.start()

    er[o] = emb[0]
    wr1[me] = pay[me]

    def arrived(dst, sem):
        pltpu.make_async_copy(dst, dst, sem).wait()

    def total(buf):
        acc = buf[0]
        for n in range(1, 16):
            acc = acc + buf[n]
        return acc

    for n in range(1, 16):
        other, _t = peer_a(n)
        arrived(wr1.at[other], r1.at[other])
    w2[...] = total(wr1)
    second = [remote(w2, wr2.at[b], s2.at[n], r2.at[b], target)
              for n in range(1, 16) for other, target in [peer_b(n)]]
    for c in second:
        c.start()
    wr2[b] = w2[...]
    for n in range(1, 16):
        other, _t = peer_b(n)
        arrived(wr2.at[other], r2.at[other])
    res[me] = total(wr2)
    third = [remote(res.at[me], res.at[me], s3.at[n], r3.at[me], target)
             for n in range(1, 16) for other, target in [peer_a(n)]]
    for c in third:
        c.start()

    for kind in range(3):
        for n in range(8):
            if kind == 0 and n == 0:
                continue
            oo = lax.rem(o + n, 8)
            slot = kind * 8 + oo
            if kind == 1 and n == 0:
                @pl.when(o > 0)
                def _():
                    arrived(er.at[slot], erc.at[slot])
            else:
                arrived(er.at[slot], erc.at[slot])

    @pl.when(o == 0)
    def _():
        local.wait()

    acc = er[0]
    for n in range(1, 24):
        acc = acc + er[n]
    emb_out[...] = acc
    for n in range(1, 16):
        other, _t = peer_a(n)
        arrived(res.at[other], r3.at[other])
    unpack_grads(res, gw_out, gb_out)
    for c in first + second + third + eout:
        c.wait_send()

    @pl.when(o > 0)
    def _():
        own.wait_send()


def per_device(bin_embed, weights, biases, dilations, cotangent):
    vmem = pl.BlockSpec(memory_space=pltpu.VMEM)
    smem = pl.BlockSpec(memory_space=pltpu.SMEM)
    shape = jax.ShapeDtypeStruct
    dma = pltpu.SemaphoreType.DMA
    ec, er, a, rl, rr = pl.pallas_call(
        exchange_kernel,
        out_shape=[shape((6, CH, 128), bf16), shape((3, CH, 128), bf16), shape((H2, CH, 128), bf16),
                   shape((40, CH, 128), bf16), shape((40, CH, 128), bf16)],
        in_specs=[vmem] * 2,
        out_specs=[vmem] * 5,
        scratch_shapes=[pltpu.VMEM((32, CH, 128), bf16), pltpu.VMEM((32, CH, 128), bf16),
                        dma((6,)), dma((6,)), dma((8,)), dma((8,))],
        compiler_params=pltpu.CompilerParams(collective_id=0, has_side_effects=True, vmem_limit_bytes=32 << 20),
        name="exchange",
    )(bin_embed, cotangent)
    out, pay, emb = pl.pallas_call(
        compute_kernel,
        out_shape=[shape((CH, TI, TK), bf16), shape((16, 2, 8, 128), f32), shape((3, CH, 128), f32)],
        in_specs=[smem] + [vmem] * 7,
        out_specs=[vmem] * 3,
        scratch_shapes=[pltpu.VMEM((H2, CH, 256), bf16), pltpu.VMEM((H1, CH, 256), bf16),
                        pltpu.VMEM((H2, 5 * CH, 256), bf16), pltpu.VMEM((H2, 5 * CH, 256), bf16),
                        pltpu.VMEM((H1, 5 * CH, 128), bf16), pltpu.VMEM((H1, 5 * CH, 128), bf16),
                        pltpu.VMEM((2, CH, 9 * CH), bf16), pltpu.VMEM((2, CH, 9 * CH), bf16),
                        pltpu.VMEM((CH, 9 * CH), f32), pltpu.VMEM((CH, 128), f32)],
        compiler_params=pltpu.CompilerParams(vmem_limit_bytes=63 << 20),
        name="compute",
    )(dilations, ec, er, a, rl, rr, weights, biases)
    gw, gb, ge = pl.pallas_call(
        reduce_kernel,
        out_shape=[shape((2, 9, CH, CH), f32), shape((2, CH), f32), shape((CH, TI), f32)],
        in_specs=[vmem] * 2,
        out_specs=[vmem] * 3,
        scratch_shapes=[pltpu.VMEM((16, 2, 8, 128), f32), pltpu.VMEM((2, 8, 128), f32),
                        pltpu.VMEM((16, 2, 8, 128), f32), pltpu.VMEM((16, 2, 8, 128), f32),
                        pltpu.VMEM((24, CH, 128), f32),
                        dma((16,)), dma((16,)), dma((16,)), dma((16,)), dma((16,)), dma((16,)),
                        dma((24,)), dma((24,)), dma],
        compiler_params=pltpu.CompilerParams(collective_id=1, has_side_effects=True, vmem_limit_bytes=32 << 20),
        name="reduce",
    )(pay, emb)
    return out, gw, gb, ge


def solution(mesh):
    placed = (P(None, "diag"), P(), P(), P(), P(None, "diag", "off"))
    return jax.shard_map(
        per_device,
        mesh=mesh,
        in_specs=placed,
        out_specs=(P(None, "diag", "off"), P(), P(), P(None, "diag")),
        check_vma=False,
    )
```

time: 679 us -> 121 us (0.18); the launches traced: 668 us -> 121 us
  waiting for transfers between devices: 273 us -> 0 us
  Pallas kernels: 0 us -> 111 us
  starting transfers between devices: 101 us -> 0 us
  local copies, waits for them, and re-layouts: 109 us -> 9.24 us
  blocking collectives: 90.8 us -> 0 us
  matrix products: 40.1 us -> 0 us
  other arithmetic: 28.9 us -> 0 us
  between operations: 25 us -> 0.67 us
    psum x2 -> x0, waiting for transfers between devices: 261 us -> none  [the longest x1 211 us: per_device(): lax.psum((jnp.stack(weight_grads), jnp.stack(bias_grads)), ('diag', 'off'))]
    pallas_call x0 -> x3, Pallas kernels: none -> 111 us  [the longest x1 47.7 us: per_device(): pl.pallas_call(compute_kernel, out_shape=[shape((CH, TI, TK), bf16), shap...]
    ppermute x32 -> x0, starting transfers between devices: 101 us -> none  [the longest x16 51.1 us: from_behind(): return lax.ppermute(block, axis, route)]
    psum x1 -> x0, blocking collectives: 90.8 us -> none  [per_device(): lax.psum((jnp.stack(weight_grads), jnp.stack(bias_grads)), ('diag', 'off'))]
    dot_general x18 -> x0, matrix products: 40.1 us -> none  [the longest x12 33.1 us: tap_sum(): jnp.einsum('oc,chw->ohw', joined, stacked, preferred_element_type=jnp.flo...]
    slice x22 -> x0, local copies, waits for them, and re-layouts: 30.9 us -> none  [the longest x12 16.2 us: extended(): last = lax.slice_in_dim(array, length - width, length, axis=dim)]
    ppermute x8 -> x0, local copies, waits for them, and re-layouts: 26 us -> none  [the longest x4 14 us: extended(): after = lax.ppermute(first, axis, down)]
    dynamic_slice x5 -> x0, local copies, waits for them, and re-layouts: 18.7 us -> none  [the longest x4 18.7 us: row_taps(): lax.dynamic_slice(source, (anchor, start_row, start_band), (channels, row...]
  transfers between devices with their start and end apart: 34 -> 0, of which waited for: 5 -> 0; matrix products, arithmetic and copies ran while one was open for 20% -> 0% of each run, Pallas kernels for 0% -> 0%
where the time goes in v1:
time: 121 us
  Pallas kernels  111 us (92%)
  local copies, waits for them, and re-layouts  9.24 us (8%)
    pallas_call x1, Pallas kernels, per_device(): pl.pallas_call(compute_kernel, out_shape=[shape((CH, TI, TK), bf16), shap...  47.7 us
    pallas_call x1, Pallas kernels, per_device(): pl.pallas_call(exchange_kernel, out_shape=[shape((6, CH, 128), bf16), sha...  32.8 us
    pallas_call x1, Pallas kernels, per_device(): pl.pallas_call(reduce_kernel, out_shape=[shape((2, 9, CH, CH), f32), shap...  30.1 us
    unnamed x21, local copies, waits for them, and re-layouts  9.24 us

profile of v1, /device:TPU:1, one launch (start us, length us, event | category | flops | bytes accessed | tf_op | source)
XLA Modules:
  0.0 120.6 jit_solution(914095885545662469)
XLA Ops:
  0.6 0.0 copy-start.1
  0.6 1.2 %copy-done.1 = bf16[32,128,128]{2,1,0:T(8,128)(2,1)S(1)} copy-done((bf16[32,128,128]{2,1,0:T(8,128)(2,1)S(1)}, bf16[32,128,128]{2,1,0:T(8,128)(2,1)}, u32[]{:S(2)}) %copy-start.1) | copy-done | bytes 1048600
  1.9 0.0 copy-start.8
  1.9 0.7 copy-done.8
  2.6 32.8 %exchange.1 = (bf16[6,32,128]{2,1,0:T(8,128)(2,1)S(1)}, bf16[3,32,128]{2,1,0:T(8,128)(2,1)S(1)}, bf16[160,32,128]{2,1,0:T(8,128)(2,1)S(1)}, bf16[40,32,128]{2,1,0:T(8,128)(2,1)S(1)}, bf16[40,32,128]{2,1,0:T(8,128)(2,1)S(1)}) custom-call(bf16[32,128]{1,0:T(8,128)(2,1)S(1)} %copy-done.8, bf16[32,128,128]{2,1,0:T(8,128)(2,1)S(1)} %copy-done.1), custom_call_target="tpu_custom_call" | custom-call | tf_op jit(solution)/shard_map/exchange/pallas_call | solution.py:521
  35.4 0.0 copy-start
  35.4 1.1 copy-done
  36.5 0.0 copy-start.2
  36.5 0.7 copy-done.2
  37.2 0.0 copy-start.3
  37.2 0.7 copy-done.3
  37.9 0.0 copy-start.6
  37.9 0.6 copy-done.6
  38.5 0.0 copy-start.7
  38.5 0.6 copy-done.7
  39.1 47.7 %compute.1 = (bf16[32,128,128]{2,1,0:T(8,128)(2,1)}, f32[16,2,8,128]{3,2,1,0:T(8,128)}, f32[3,32,128]{2,1,0:T(8,128)}) custom-call(s32[2]{0:T(128)} %dil.1, bf16[6,32,128]{2,1,0:T(8,128)(2,1)} %copy-done.6, bf16[3,32,128]{2,1,0:T(8,128)(2,1)} %copy-done.7, bf16[160,32,128]{2,1,0:T(8,128)(2,1)} %copy-done, bf16[40,32,128]{2,1,0:T(8,128)(2,1)} %copy-done.2, ...), custom_call_target="tpu_custom_call" | custom-call | tf_op jit(solution)/shard_map/compute/pallas_call | solution.py:532
  86.9 0.0 copy-start.4
  86.9 0.9 copy-done.4
  87.8 0.0 copy-start.5
  87.8 0.8 copy-done.5
  88.6 30.1 %reduce.1 = (f32[2,9,32,32]{3,2,1,0:T(8,128)S(1)}, f32[2,32]{1,0:T(2,128)S(1)}, f32[32,128]{1,0:T(8,128)S(1)}) custom-call(f32[16,2,8,128]{3,2,1,0:T(8,128)S(1)} %copy-done.4, f32[3,32,128]{2,1,0:T(8,128)S(1)} %copy-done.5), custom_call_target="tpu_custom_call" | custom-call | tf_op jit(solution)/shard_map/reduce/pallas_call | solution.py:545
  118.7 0.7 copy.12
  119.4 0.6 copy.13
  120.0 0.6 copy.14
Async XLA Ops:
  0.6 1.2 %copy-start.1 = (bf16[32,128,128]{2,1,0:T(8,128)(2,1)S(1)}, bf16[32,128,128]{2,1,0:T(8,128)(2,1)}, u32[]{:S(2)}) copy-start(bf16[32,128,128]{2,1,0:T(8,128)(2,1)} %cot.1) | copy-start | bytes 3145732
  1.9 0.7 copy-start.8
  35.4 1.1 copy-start
  36.5 0.7 copy-start.2
  37.2 0.7 copy-start.3
  37.9 0.6 copy-start.6
  38.5 0.6 copy-start.7
  86.9 0.9 copy-start.4
  87.8 0.8 copy-start.5

commit v2 on v1

--- a/solution.py
+++ b/solution.py
@@ -341,62 +341,18 @@
     lax.fori_loop(0, 8, body, 0)
 
 
-def exchange_kernel(emb, cot, ec, er, a, rl, rr, pl_, pr_, esend, erecv, hsend, hrecv):
-    r, o = lax.axis_index("diag"), lax.axis_index("off")
-    barrier = pltpu.get_barrier_semaphore()
-    count = greet_exchange(r, o, barrier)
-    ec[0] = jnp.zeros((CH, 128), bf16)
-    ec[5] = jnp.zeros((CH, 128), bf16)
-    er[1] = emb[...]
-    pl.semaphore_wait(barrier, count)
-    ecopies = embed_copies(r, o, emb, ec, er, esend, erecv)
-    for c in ecopies:
-        c.start()
-    lay_rows(cot, a, pl_, pr_)
-    hcopies = halo_copies(r, o, a, pl_, pr_, rl, rr, hsend, hrecv)
-    for c in hcopies:
-        c.start()
-    for c in ecopies + hcopies:
-        c.wait()
-
-
-def compute_kernel(
-    dil, ec, er, a_rows, rl, rr, w, bias, out, pay, emb, x0, x1, s0, t1, s1, t0, wf, wb, gw, gb
-):
-    r, o = lax.axis_index("diag"), lax.axis_index("off")
-    d0, d1 = dil[0], dil[1]
-    row0, band0 = r * TI, o * TK
-    place_weights(w, wf, wb)
-    eye = lax.broadcasted_iota(jnp.int32, (CH, CH), 0) == lax.broadcasted_iota(jnp.int32, (CH, CH), 1)
-
-    def column(layer):
-        return jnp.sum(jnp.where(eye, bias[layer : layer + 1, :], 0.0), axis=1, keepdims=True)
-
-    phase_x0(row0, band0, d0, ec, er, x0, s0, 8)
-    phase_x1(row0, band0, d0, d1, wf[0], column(0), x0, s0, x1, s1, 16)
-    phase_x2(row0, band0, d1, wf[1], column(1), x1, s1, out, 32)
-    phase_h(row0, band0, d1, a_rows, rl, rr, t1)
-    phase_gw(t1, 16, s1, 8, d1, gw, gb, 16)
-    third1 = pack_grads(1, gw, gb, pay)
-    phase_g1(d1, d0, wb[1], x1, t1, t0, 16)
-    phase_gw(t0, 8, s0, 16, d0, gw, gb, 16)
-    third0 = pack_grads(0, gw, gb, pay)
-    third = third0 + pltpu.roll(third1, 64, 1)
-    for n in range(16):
-        pay[n, 1] = third[8 * n : 8 * n + 8] if n < 4 else jnp.zeros((8, 128), f32)
-    rsum, lo, hi = phase_g0(d0, wb[0], x0, t0, 16)
-    emb[0] = rsum
-    emb[1] = lo
-    emb[2] = hi
-
-
-def reduce_kernel(
-    pay, emb, gw_out, gb_out, emb_out, wr1, w2, wr2, res, er, s1, r1, s2, r2, s3, r3, es, erc, ls
+def kernel(
+    dil, emb, w, bias, cot_hbm, out_hbm, gw_out, gb_out, ge_out,
+    cot, out, ec, er, a, rl, rr, pl_, pr_, x0, x1, s0, t1, s1, t0, wf, wb, gw, gb,
+    pay, terms, wr1, w2, wr2, res, inbox,
+    io, esend, erecv, hsend, hrecv, sa, ra, sb, rb, sc, rc, st, rt, local_sem,
 ):
     r, o = lax.axis_index("diag"), lax.axis_index("off")
     core, b = lax.rem(r, 2), lax.div(r, 2)
     me = o * 2 + core
-    barrier = pltpu.get_barrier_semaphore()
+    row0, band0 = r * TI, o * TK
+    fetch = pltpu.make_async_copy(cot_hbm, cot, io.at[0])
+    fetch.start()
 
     def peer_a(n):
         other = lax.rem(me + n, 16)
@@ -406,15 +362,17 @@
         other = lax.rem(b + n, 16)
         return other, (2 * other + core, o)
 
+    barrier = pltpu.get_barrier_semaphore()
+
     def greet(target):
         pl.semaphore_signal(barrier, inc=1, device_id=target, device_id_type=MESH)
 
+    count = greet_exchange(r, o, barrier)
     for n in range(1, 16):
         greet(peer_a(n)[1])
         greet(peer_b(n)[1])
     for n in range(1, 8):
         oo = lax.rem(o + n, 8)
-        greet(wrap(r, oo))
         greet(wrap(r - oo, oo))
         greet(wrap(r - oo - 1, oo))
     greet(wrap(r - o - 1, o))
@@ -423,35 +381,72 @@
     def _():
         greet(wrap(r - o, o))
 
-    pl.semaphore_wait(barrier, 30 + 21 + 1 + jnp.minimum(o, 1))
-
-    first = [remote(pay.at[other], wr1.at[me], s1.at[n], r1.at[me], target)
+    count = count + 30 + 14 + 1 + jnp.minimum(o, 1)
+    ec[0] = jnp.zeros((CH, 128), bf16)
+    ec[5] = jnp.zeros((CH, 128), bf16)
+    er[1] = emb[...]
+    place_weights(w, wf, wb)
+    fetch.wait()
+    lay_rows(cot, a, pl_, pr_)
+    pl.semaphore_wait(barrier, count)
+    ecopies = embed_copies(r, o, emb, ec, er, esend, erecv)
+    hcopies = halo_copies(r, o, a, pl_, pr_, rl, rr, hsend, hrecv)
+    for c in ecopies + hcopies:
+        c.start()
+
+    eye = lax.broadcasted_iota(jnp.int32, (CH, CH), 0) == lax.broadcasted_iota(jnp.int32, (CH, CH), 1)
+
+    def column(layer):
+        return jnp.sum(jnp.where(eye, bias[layer : layer + 1, :], 0.0), axis=1, keepdims=True)
+
+    d0, d1 = dil[0], dil[1]
+    for c in ecopies:
+        c.wait_recv()
+    phase_x0(row0, band0, d0, ec, er, x0, s0, 8)
+    phase_x1(row0, band0, d0, d1, wf[0], column(0), x0, s0, x1, s1, 16)
+    for c in hcopies:
+        c.wait_recv()
+    phase_h(row0, band0, d1, a, rl, rr, t1)
+    phase_g1(d1, d0, wb[1], x1, t1, t0, 16)
+    phase_gw(t1, 16, s1, 8, d1, gw, gb, 16)
+    third1 = pack_grads(1, gw, gb, pay)
+    phase_gw(t0, 8, s0, 16, d0, gw, gb, 16)
+    third0 = pack_grads(0, gw, gb, pay)
+    rest = third0 + pltpu.roll(third1, 64, 1)
+    for n in range(16):
+        pay[n, 1] = rest[8 * n : 8 * n + 8] if n < 4 else jnp.zeros((8, 128), f32)
+
+    first = [remote(pay.at[other], wr1.at[me], sa.at[n], ra.at[me], target)
              for n in range(1, 16) for other, target in [peer_a(n)]]
     for c in first:
         c.start()
+
+    rsum, lo, hi = phase_g0(d0, wb[0], x0, t0, 16)
+    terms[0] = rsum
+    terms[1] = lo
+    terms[2] = hi
     eout = []
     for n in range(0, 8):
         oo = lax.rem(o + n, 8)
         for kind, dr in ((0, 0), (1, o), (2, o + 1)):
             if n == 0 and kind < 2:
                 continue
-            eout.append(remote(emb.at[kind], er.at[kind * 8 + o], es.at[kind * 8 + n], erc.at[kind * 8 + o], wrap(r + dr, oo)))
+            eout.append(remote(terms.at[kind], inbox.at[kind * 8 + o], st.at[kind * 8 + n], rt.at[kind * 8 + o], wrap(r + dr, oo)))
     for c in eout:
         c.start()
-    own = remote(emb.at[1], er.at[8 + o], es.at[8], erc.at[8 + o], wrap(r + o, o))
+    own = remote(terms.at[1], inbox.at[8 + o], st.at[8], rt.at[8 + o], wrap(r + o, o))
 
     @pl.when(o > 0)
     def _():
         own.start()
 
-    local = pltpu.make_async_copy(emb.at[1], er.at[8 + o], ls)
+    local = pltpu.make_async_copy(terms.at[1], inbox.at[8 + o], local_sem)
 
     @pl.when(o == 0)
     def _():
         local.start()
 
-    er[o] = emb[0]
-    wr1[me] = pay[me]
+    inbox[o] = terms[0]
 
     def arrived(dst, sem):
         pltpu.make_async_copy(dst, dst, sem).wait()
@@ -462,20 +457,26 @@
             acc = acc + buf[n]
         return acc
 
+    wr1[me] = pay[me]
     for n in range(1, 16):
         other, _t = peer_a(n)
-        arrived(wr1.at[other], r1.at[other])
+        arrived(wr1.at[other], ra.at[other])
     w2[...] = total(wr1)
-    second = [remote(w2, wr2.at[b], s2.at[n], r2.at[b], target)
+    second = [remote(w2, wr2.at[b], sb.at[n], rb.at[b], target)
               for n in range(1, 16) for other, target in [peer_b(n)]]
     for c in second:
         c.start()
+
+    phase_x2(row0, band0, d1, wf[1], column(1), x1, s1, out, 32)
+    write = pltpu.make_async_copy(out, out_hbm, io.at[1])
+    write.start()
+
     wr2[b] = w2[...]
     for n in range(1, 16):
         other, _t = peer_b(n)
-        arrived(wr2.at[other], r2.at[other])
+        arrived(wr2.at[other], rb.at[other])
     res[me] = total(wr2)
-    third = [remote(res.at[me], res.at[me], s3.at[n], r3.at[me], target)
+    third = [remote(res.at[me], res.at[me], sc.at[n], rc.at[me], target)
              for n in range(1, 16) for other, target in [peer_a(n)]]
     for c in third:
         c.start()
@@ -489,73 +490,64 @@
             if kind == 1 and n == 0:
                 @pl.when(o > 0)
                 def _():
-                    arrived(er.at[slot], erc.at[slot])
+                    arrived(inbox.at[slot], rt.at[slot])
             else:
-                arrived(er.at[slot], erc.at[slot])
+                arrived(inbox.at[slot], rt.at[slot])
 
     @pl.when(o == 0)
     def _():
         local.wait()
 
-    acc = er[0]
+    acc = inbox[0]
     for n in range(1, 24):
-        acc = acc + er[n]
-    emb_out[...] = acc
+        acc = acc + inbox[n]
+    ge_out[...] = acc
     for n in range(1, 16):
         other, _t = peer_a(n)
-        arrived(res.at[other], r3.at[other])
+        arrived(res.at[other], rc.at[other])
     unpack_grads(res, gw_out, gb_out)
-    for c in first + second + third + eout:
+    for c in first + second + third + eout + ecopies + hcopies:
         c.wait_send()
 
     @pl.when(o > 0)
     def _():
         own.wait_send()
 
+    write.wait()
+
 
 def per_device(bin_embed, weights, biases, dilations, cotangent):
     vmem = pl.BlockSpec(memory_space=pltpu.VMEM)
     smem = pl.BlockSpec(memory_space=pltpu.SMEM)
+    hbm = pl.BlockSpec(memory_space=pl.ANY)
     shape = jax.ShapeDtypeStruct
     dma = pltpu.SemaphoreType.DMA
-    ec, er, a, rl, rr = pl.pallas_call(
-        exchange_kernel,
-        out_shape=[shape((6, CH, 128), bf16), shape((3, CH, 128), bf16), shape((H2, CH, 128), bf16),
-                   shape((40, CH, 128), bf16), shape((40, CH, 128), bf16)],
-        in_specs=[vmem] * 2,
-        out_specs=[vmem] * 5,
-        scratch_shapes=[pltpu.VMEM((32, CH, 128), bf16), pltpu.VMEM((32, CH, 128), bf16),
-                        dma((6,)), dma((6,)), dma((8,)), dma((8,))],
-        compiler_params=pltpu.CompilerParams(collective_id=0, has_side_effects=True, vmem_limit_bytes=32 << 20),
-        name="exchange",
-    )(bin_embed, cotangent)
-    out, pay, emb = pl.pallas_call(
-        compute_kernel,
-        out_shape=[shape((CH, TI, TK), bf16), shape((16, 2, 8, 128), f32), shape((3, CH, 128), f32)],
-        in_specs=[smem] + [vmem] * 7,
-        out_specs=[vmem] * 3,
-        scratch_shapes=[pltpu.VMEM((H2, CH, 256), bf16), pltpu.VMEM((H1, CH, 256), bf16),
-                        pltpu.VMEM((H2, 5 * CH, 256), bf16), pltpu.VMEM((H2, 5 * CH, 256), bf16),
-                        pltpu.VMEM((H1, 5 * CH, 128), bf16), pltpu.VMEM((H1, 5 * CH, 128), bf16),
-                        pltpu.VMEM((2, CH, 9 * CH), bf16), pltpu.VMEM((2, CH, 9 * CH), bf16),
-                        pltpu.VMEM((CH, 9 * CH), f32), pltpu.VMEM((CH, 128), f32)],
-        compiler_params=pltpu.CompilerParams(vmem_limit_bytes=63 << 20),
-        name="compute",
-    )(dilations, ec, er, a, rl, rr, weights, biases)
-    gw, gb, ge = pl.pallas_call(
-        reduce_kernel,
-        out_shape=[shape((2, 9, CH, CH), f32), shape((2, CH), f32), shape((CH, TI), f32)],
-        in_specs=[vmem] * 2,
-        out_specs=[vmem] * 3,
-        scratch_shapes=[pltpu.VMEM((16, 2, 8, 128), f32), pltpu.VMEM((2, 8, 128), f32),
-                        pltpu.VMEM((16, 2, 8, 128), f32), pltpu.VMEM((16, 2, 8, 128), f32),
-                        pltpu.VMEM((24, CH, 128), f32),
-                        dma((16,)), dma((16,)), dma((16,)), dma((16,)), dma((16,)), dma((16,)),
-                        dma((24,)), dma((24,)), dma],
-        compiler_params=pltpu.CompilerParams(collective_id=1, has_side_effects=True, vmem_limit_bytes=32 << 20),
-        name="reduce",
-    )(pay, emb)
-    return out, gw, gb, ge
+    mem = pltpu.VMEM
+    return pl.pallas_call(
+        kernel,
+        out_shape=[shape((CH, TI, TK), bf16), shape((2, 9, CH, CH), f32), shape((2, CH), f32), shape((CH, TI), f32)],
+        in_specs=[smem, vmem, vmem, vmem, hbm],
+        out_specs=[hbm, vmem, vmem, vmem],
+        scratch_shapes=[
+            mem((CH, TI, TK), bf16), mem((CH, TI, TK), bf16),
+            mem((6, CH, 128), bf16), mem((3, CH, 128), bf16), mem((H2, CH, 128), bf16),
+            mem((40, CH, 128), bf16), mem((40, CH, 128), bf16),
+            mem((32, CH, 128), bf16), mem((32, CH, 128), bf16),
+            mem((H2, CH, 256), bf16), mem((H1, CH, 256), bf16),
+            mem((H2, 5 * CH, 256), bf16), mem((H2, 5 * CH, 256), bf16),
+            mem((H1, 5 * CH, 128), bf16), mem((H1, 5 * CH, 128), bf16),
+            mem((2, CH, 9 * CH), bf16), mem((2, CH, 9 * CH), bf16),
+            mem((CH, 9 * CH), f32), mem((CH, 128), f32),
+            mem((16, 2, 8, 128), f32), mem((3, CH, 128), f32),
+            mem((16, 2, 8, 128), f32), mem((2, 8, 128), f32),
+            mem((16, 2, 8, 128), f32), mem((16, 2, 8, 128), f32), mem((24, CH, 128), f32),
+            dma((2,)), dma((6,)), dma((6,)), dma((8,)), dma((8,)),
+            dma((16,)), dma((16,)), dma((16,)), dma((16,)), dma((16,)), dma((16,)),
+            dma((24,)), dma((24,)), dma,
+        ],
+        compiler_params=pltpu.CompilerParams(collective_id=0, has_side_effects=True, vmem_limit_bytes=63 << 20),
+        name="section",
+    )(dilations, bin_embed, weights, biases, cotangent)
 
 
 def solution(mesh):

time: 121 us -> 91.5 us (0.76)
  Pallas kernels: 111 us -> 86.4 us
  local copies, waits for them, and re-layouts: 9.24 us -> 4.24 us
    pallas_call x3 -> x1, Pallas kernels: 111 us -> 86.4 us  [per_device(): pl.pallas_call(kernel, out_shape=[shape((CH, TI, TK), bf16), shape((2, 9,...]
    unnamed x21 -> x10, local copies, waits for them, and re-layouts: 9.24 us -> 4.24 us
where the time goes in v2:
time: 91.5 us; the launch traced here: 91.3 us
  Pallas kernels  86.4 us (94%)
  local copies, waits for them, and re-layouts  4.24 us (5%)
    pallas_call x1, Pallas kernels, per_device(): pl.pallas_call(kernel, out_shape=[shape((CH, TI, TK), bf16), shape((2, 9,...  86.4 us
    unnamed x10, local copies, waits for them, and re-layouts  4.24 us

profile of v2, /device:TPU:1, one launch (start us, length us, event | category | flops | bytes accessed | tf_op | source)
XLA Modules:
  0.0 91.3 jit_solution(9396014032516114600)
XLA Ops:
  0.6 86.4 %section.1 = (bf16[32,128,128]{2,1,0:T(8,128)(2,1)}, f32[2,9,32,32]{3,2,1,0:T(8,128)}, f32[2,32]{1,0:T(2,128)}, f32[32,128]{1,0:T(8,128)}) custom-call(s32[2]{0:T(128)} %dil.1, bf16[32,128]{1,0:T(8,128)(2,1)} %emb.1, bf16[2,9,32,32]{3,2,1,0:T(8,128)(2,1)} %w.1, f32[2,32]{1,0:T(2,128)} %bias.1, bf16[32,128,128]{2,1,0:T(8,128)(2,1)} %cot_hbm.1), custom_call_target="tpu_custom_call" | custom-call | tf_op jit(solution)/shard_map/section/pallas_call | solution.py:526
  87.1 0.0 copy-start
  87.1 2.4 %copy.13 = bf16[32,128,128]{2,1,0:T(8,128)(2,1)} copy(bf16[32,128,128]{2,1,0:T(8,128)(2,1)} %get-tuple-element.8) | data formatting | bytes 2097152
  89.4 0.0 copy-done
  89.4 0.0 copy-start.2
  89.4 0.0 copy-start.1
  89.4 0.7 copy.14
  90.2 0.0 copy-done.2
  90.2 0.6 copy.15
  90.7 0.0 copy-done.1
  90.7 0.6 copy.16
Async XLA Ops:
  87.1 2.4 %copy-start = (f32[2,9,32,32]{3,2,1,0:T(8,128)S(1)}, f32[2,9,32,32]{3,2,1,0:T(8,128)}, u32[]{:S(2)}) copy-start(f32[2,9,32,32]{3,2,1,0:T(8,128)} %get-tuple-element.9) | copy-start | bytes 221188
  89.4 0.7 copy-start.2
  89.4 1.3 %copy-start.1 = (f32[32,128]{1,0:T(8,128)S(1)}, f32[32,128]{1,0:T(8,128)}, u32[]{:S(2)}) copy-start(f32[32,128]{1,0:T(8,128)} %get-tuple-element.11) | copy-start | bytes 49156

commit v3 on v2

--- a/solution.py
+++ b/solution.py
@@ -146,7 +146,7 @@
     lax.fori_loop(0, TI // unroll, body, 0)
 
 
-def phase_gw(h, hoff, s, soff, d, gw, gb, unroll=4):
+def phase_gw(h, s, soff, d, gw, gb, unroll=16):
     def body(it, carry):
         acc, accb = carry
         for w in range(0, unroll, 2):
@@ -154,8 +154,7 @@
             x = jnp.concatenate(
                 [taps(s, i + soff, d, 0, 128), taps(s, i + 1 + soff, d, 0, 128)], axis=1
             )
-            ha = h[i + hoff, 64:96, 0:128]
-            hb = h[i + hoff + 1, 64:96, 0:128]
+            ha, hb = h(i), h(i + 1)
             hh = jnp.concatenate([ha, hb], axis=1)
             acc = acc + lax.dot_general(hh, x, NT, preferred_element_type=f32)
             accb = accb + (ha.astype(f32) + hb.astype(f32))
@@ -168,43 +167,68 @@
     gb[...] = accb
 
 
-def phase_h(row0, band0, d, a_rows, rl, rr, t1):
-    amounts, insides = shift_tables(d)
+def packed(rows):
+    lane = lanes()
+    left, right = rows[0], rows[7]
+    for w in range(1, 8):
+        left = jnp.where(lane < 16 * w, left, pltpu.roll(rows[w], 16 * w, 1))
+    for w in range(6, -1, -1):
+        right = jnp.where(lane >= 16 * (w + 1), right, pltpu.roll(rows[w], 16 * w + 16, 1))
+    return left, right
+
+
+def phase_shift(row0, band0, d, rows, rl, rr, dst, unroll=2):
+    lane = lanes()
+    insides = [in_range(s * d) for s in (-2, -1, 1, 2)]
 
     def body(it, _):
-        pl_, pr_ = rl[it], rr[it]
-        for w in range(4):
-            j = it * 4 + w
-            ma, mb = row_masks(row0, band0, j - 2 * DMAX)
-            right = pltpu.roll(pl_, (128 - 32 * w) % 128, 1) if w else pl_
-            left = pltpu.roll(pr_, 32 * (3 - w), 1) if w < 3 else pr_
-            b = jnp.where(lanes() < 64, right, left)
-            a = jnp.where(ma, a_rows[j], 0)
-            b = jnp.where(mb, b, 0)
-            store_shifts(t1, j, a, b, amounts, insides)
+        for g in range(unroll):
+            group = it * unroll + g
+            first = row0 + group * 8 - DMAX
+            row = first + lax.div(lane, 16)
+            kr = band0 + 128 + lax.rem(lane, 16)
+            kl = band0 - 16 + lax.rem(lane, 16)
+            right = jnp.where((row >= 0) & (kr < KBAND) & (kr < NBINS - row), rl[group], 0)
+            left = jnp.where((row >= 0) & (kl >= 0) & (kl < NBINS - row), rr[group], 0)
+            for w in range(8):
+                j = group * 8 + w
+                live = (first + w >= 0) & (band0 + lane < NBINS - (first + w))
+                a = jnp.where(live, rows[j], 0)
+                dst[j, 64:96, :] = a
+                for n, s in enumerate((-2, -1, 1, 2)):
+                    if s > 0:
+                        side = pltpu.roll(right, lax.rem(256 - 16 * w - s * d, 128), 1)
+                    else:
+                        side = pltpu.roll(left, lax.rem(256 + 16 * (7 - w) - s * d, 128), 1)
+                    m = n if s < 0 else n + 1
+                    dst[j, CH * m : CH * m + CH, :] = jnp.where(
+                        insides[n], pltpu.roll(a, lax.rem(256 - s * d, 128), 1), side
+                    )
         return 0
 
-    lax.fori_loop(0, H2 // 4, body, 0)
-
-
-def phase_g1(d, dn, wb, x1, t1, t0, unroll=4):
-    amounts, insides = shift_tables(dn)
-
+    lax.fori_loop(0, H1 // 8 // unroll, body, 0)
+
+
+def phase_g1(d, wb, x1, t1, ga, gpl, gpr, unroll=16):
     def body(it, _):
-        for w in range(unroll):
-            j = it * unroll + w
-            jj = j + DMAX
-            q = jnp.dot(wb, taps(t1, jj, d), preferred_element_type=f32)
-            ab = []
+        rows = []
+        for w in range(0, unroll, 2):
+            j = it * unroll + w + DMAX
+            x = jnp.concatenate([taps(t1, j, d, 0, 128), taps(t1, j + 1, d, 0, 128)], axis=1)
+            q = jnp.dot(wb, x, preferred_element_type=f32)
             for z in range(2):
-                sl = slice(128 * z, 128 * z + 128)
-                h = t1[jj, 64:96, sl].astype(f32)
-                gate = x1[j, :, sl].astype(f32) > 0
-                ab.append((h + jnp.where(gate, q[:, sl], 0.0)).astype(bf16))
-            store_shifts(t0, j, ab[0], ab[1], amounts, insides, False)
+                h = t1[j + z, 64:96, :].astype(f32)
+                gate = x1[j + z, :, 0:128].astype(f32) > 0
+                g = (h + jnp.where(gate, q[:, 128 * z : 128 * z + 128], 0.0)).astype(bf16)
+                ga[j + z] = g
+                rows.append(g)
+        for n in range(unroll // 8):
+            left, right = packed(rows[8 * n : 8 * n + 8])
+            gpl[it * (unroll // 8) + n] = left
+            gpr[it * (unroll // 8) + n] = right
         return 0
 
-    lax.fori_loop(0, H1 // unroll, body, 0)
+    lax.fori_loop(0, TI // unroll, body, 0)
 
 
 def phase_g0(d, wb, x0, t0, unroll=4):
@@ -284,16 +308,15 @@
 
 
 def halo_copies(r, o, a, pl_, pr_, rl, rr, send, recv):
-    last, first = slice(112, 128), slice(0, 16)
     jobs = [
-        (a.at[16 + 112 : 16 + 128], a.at[0:16], 1, 0),
-        (a.at[16:32], a.at[144:160], -1, 0),
-        (pl_, rl.at[4:36], 0, -1),
-        (pr_, rr.at[4:36], 0, 1),
-        (pl_.at[28:32], rl.at[0:4], 1, -1),
-        (pl_.at[0:4], rl.at[36:40], -1, -1),
-        (pr_.at[28:32], rr.at[0:4], 1, 1),
-        (pr_.at[0:4], rr.at[36:40], -1, 1),
+        (pl_, rl.at[1:17], 0, -1),
+        (pr_, rr.at[1:17], 0, 1),
+        (a.at[128:136], a.at[0:8], 1, 0),
+        (a.at[8:16], a.at[136:144], -1, 0),
+        (pl_.at[15:16], rl.at[0:1], 1, -1),
+        (pl_.at[0:1], rl.at[17:18], -1, -1),
+        (pr_.at[15:16], rr.at[0:1], 1, 1),
+        (pr_.at[0:1], rr.at[17:18], -1, 1),
     ]
     return [
         remote(src, dst, send.at[n], recv.at[n], wrap(r + dr, o + do))
@@ -322,30 +345,23 @@
 
 
 def lay_rows(cot, a, pl_, pr_):
-    lane = lanes()
-
     def body(it, _):
         block = jnp.swapaxes(cot[:, pl.ds(pl.multiple_of(it * 16, 16), 16), :], 0, 1)
-        a[pl.ds(16 + it * 16, 16)] = block
-        for n in range(4):
-            left = block[4 * n]
-            right = block[4 * n + 3]
-            for w in range(1, 4):
-                left = jnp.where(lane < 32 * w, left, pltpu.roll(block[4 * n + w], 32 * w, 1))
-            for w in range(2, -1, -1):
-                right = jnp.where(lane >= 32 * (w + 1), right, pltpu.roll(block[4 * n + w], 128 - 32 * (3 - w), 1))
-            pl_[it * 4 + n] = left
-            pr_[it * 4 + n] = right
+        a[pl.ds(DMAX + it * 16, 16)] = block
+        for n in range(2):
+            left, right = packed([block[8 * n + w] for w in range(8)])
+            pl_[it * 2 + n] = left
+            pr_[it * 2 + n] = right
         return 0
 
     lax.fori_loop(0, 8, body, 0)
 
 
 def kernel(
-    dil, emb, w, bias, cot_hbm, out_hbm, gw_out, gb_out, ge_out,
-    cot, out, ec, er, a, rl, rr, pl_, pr_, x0, x1, s0, t1, s1, t0, wf, wb, gw, gb,
-    pay, terms, wr1, w2, wr2, res, inbox,
-    io, esend, erecv, hsend, hrecv, sa, ra, sb, rb, sc, rc, st, rt, local_sem,
+    dil, emb, w, bias, cot_hbm, out_hbm, res, ge,
+    cot, out, ec, er, a, rl, rr, pl_, pr_, ga, grl, grr, gpl, gpr, x0, x1, s0, t1, s1, t0, wf, wb, gw, gb,
+    pay, terms, wr1, w2, wr2, inbox,
+    io, esend, erecv, hsend, hrecv, gsend, grecv, sa, ra, sb, rb, sc, rc, st, rt, su, ru, local_sem,
 ):
     r, o = lax.axis_index("diag"), lax.axis_index("off")
     core, b = lax.rem(r, 2), lax.div(r, 2)
@@ -406,11 +422,14 @@
     phase_x1(row0, band0, d0, d1, wf[0], column(0), x0, s0, x1, s1, 16)
     for c in hcopies:
         c.wait_recv()
-    phase_h(row0, band0, d1, a, rl, rr, t1)
-    phase_g1(d1, d0, wb[1], x1, t1, t0, 16)
-    phase_gw(t1, 16, s1, 8, d1, gw, gb, 16)
+    phase_shift(row0, band0, d1, a, rl, rr, t1)
+    phase_g1(d1, wb[1], x1, t1, ga, gpl, gpr)
+    gcopies = halo_copies(r, o, ga, gpl, gpr, grl, grr, gsend, grecv)
+    for c in gcopies:
+        c.start()
+    phase_gw(lambda i: t1[i + DMAX, 64:96, :], s1, DMAX, d1, gw, gb)
     third1 = pack_grads(1, gw, gb, pay)
-    phase_gw(t0, 8, s0, 16, d0, gw, gb, 16)
+    phase_gw(lambda i: ga[i + DMAX], s0, 2 * DMAX, d0, gw, gb)
     third0 = pack_grads(0, gw, gb, pay)
     rest = third0 + pltpu.roll(third1, 64, 1)
     for n in range(16):
@@ -421,32 +440,37 @@
     for c in first:
         c.start()
 
+    for c in gcopies:
+        c.wait_recv()
+    phase_shift(row0, band0, d0, ga, grl, grr, t0)
     rsum, lo, hi = phase_g0(d0, wb[0], x0, t0, 16)
-    terms[0] = rsum
-    terms[1] = lo
-    terms[2] = hi
+    for n in range(8):
+        rows = slice(4 * n, 4 * n + 4)
+        terms[0, n] = rsum[rows]
+        terms[1, n] = lo[rows]
+        terms[2, n] = hi[rows]
     eout = []
     for n in range(0, 8):
         oo = lax.rem(o + n, 8)
         for kind, dr in ((0, 0), (1, o), (2, o + 1)):
             if n == 0 and kind < 2:
                 continue
-            eout.append(remote(terms.at[kind], inbox.at[kind * 8 + o], st.at[kind * 8 + n], rt.at[kind * 8 + o], wrap(r + dr, oo)))
+            eout.append(remote(terms.at[kind, oo], inbox.at[kind * 8 + o], st.at[kind * 8 + n], rt.at[kind * 8 + o], wrap(r + dr, oo)))
     for c in eout:
         c.start()
-    own = remote(terms.at[1], inbox.at[8 + o], st.at[8], rt.at[8 + o], wrap(r + o, o))
+    own = remote(terms.at[1, o], inbox.at[8 + o], st.at[8], rt.at[8 + o], wrap(r + o, o))
 
     @pl.when(o > 0)
     def _():
         own.start()
 
-    local = pltpu.make_async_copy(terms.at[1], inbox.at[8 + o], local_sem)
+    local = pltpu.make_async_copy(terms.at[1, o], inbox.at[8 + o], local_sem)
 
     @pl.when(o == 0)
     def _():
         local.start()
 
-    inbox[o] = terms[0]
+    inbox[o] = terms[0, o]
 
     def arrived(dst, sem):
         pltpu.make_async_copy(dst, dst, sem).wait()
@@ -470,16 +494,6 @@
     phase_x2(row0, band0, d1, wf[1], column(1), x1, s1, out, 32)
     write = pltpu.make_async_copy(out, out_hbm, io.at[1])
     write.start()
-
-    wr2[b] = w2[...]
-    for n in range(1, 16):
-        other, _t = peer_b(n)
-        arrived(wr2.at[other], rb.at[other])
-    res[me] = total(wr2)
-    third = [remote(res.at[me], res.at[me], sc.at[n], rc.at[me], target)
-             for n in range(1, 16) for other, target in [peer_a(n)]]
-    for c in third:
-        c.start()
 
     for kind in range(3):
         for n in range(8):
@@ -501,12 +515,27 @@
     acc = inbox[0]
     for n in range(1, 24):
         acc = acc + inbox[n]
-    ge_out[...] = acc
+    ge[o] = acc
+    eall = [remote(ge.at[o], ge.at[o], su.at[n], ru.at[o], wrap(r, o + n)) for n in range(1, 8)]
+    for c in eall:
+        c.start()
+
+    wr2[b] = w2[...]
+    for n in range(1, 16):
+        other, _t = peer_b(n)
+        arrived(wr2.at[other], rb.at[other])
+    res[me] = total(wr2)
+    third = [remote(res.at[me], res.at[me], sc.at[n], rc.at[me], target)
+             for n in range(1, 16) for other, target in [peer_a(n)]]
+    for c in third:
+        c.start()
+    for n in range(1, 8):
+        oo = lax.rem(o + n, 8)
+        arrived(ge.at[oo], ru.at[oo])
     for n in range(1, 16):
         other, _t = peer_a(n)
         arrived(res.at[other], rc.at[other])
-    unpack_grads(res, gw_out, gb_out)
-    for c in first + second + third + eout + ecopies + hcopies:
+    for c in first + second + third + eout + eall + ecopies + hcopies + gcopies:
         c.wait_send()
 
     @pl.when(o > 0)
@@ -514,6 +543,15 @@
         own.wait_send()
 
     write.wait()
+
+
+def finish(section, res, ge, out, gw_out, gb_out, ge_out, sem):
+    move = pltpu.make_async_copy(section, out, sem)
+    move.start()
+    unpack_grads(res, gw_out, gb_out)
+    for n in range(8):
+        ge_out[4 * n : 4 * n + 4, :] = ge[n]
+    move.wait()
 
 
 def per_device(bin_embed, weights, biases, dilations, cotangent):
@@ -523,31 +561,39 @@
     shape = jax.ShapeDtypeStruct
     dma = pltpu.SemaphoreType.DMA
     mem = pltpu.VMEM
-    return pl.pallas_call(
+    halo = [mem((H1, CH, 128), bf16), mem((18, CH, 128), bf16), mem((18, CH, 128), bf16),
+            mem((16, CH, 128), bf16), mem((16, CH, 128), bf16)]
+    section, res, ge = pl.pallas_call(
         kernel,
-        out_shape=[shape((CH, TI, TK), bf16), shape((2, 9, CH, CH), f32), shape((2, CH), f32), shape((CH, TI), f32)],
+        out_shape=[shape((CH, TI, TK), bf16), shape((16, 2, 8, 128), f32), shape((8, 4, 128), f32)],
         in_specs=[smem, vmem, vmem, vmem, hbm],
-        out_specs=[hbm, vmem, vmem, vmem],
+        out_specs=[hbm, vmem, vmem],
         scratch_shapes=[
             mem((CH, TI, TK), bf16), mem((CH, TI, TK), bf16),
-            mem((6, CH, 128), bf16), mem((3, CH, 128), bf16), mem((H2, CH, 128), bf16),
-            mem((40, CH, 128), bf16), mem((40, CH, 128), bf16),
-            mem((32, CH, 128), bf16), mem((32, CH, 128), bf16),
+            mem((6, CH, 128), bf16), mem((3, CH, 128), bf16), *halo, *halo,
             mem((H2, CH, 256), bf16), mem((H1, CH, 256), bf16),
-            mem((H2, 5 * CH, 256), bf16), mem((H2, 5 * CH, 256), bf16),
+            mem((H2, 5 * CH, 256), bf16), mem((H1, 5 * CH, 128), bf16),
             mem((H1, 5 * CH, 128), bf16), mem((H1, 5 * CH, 128), bf16),
             mem((2, CH, 9 * CH), bf16), mem((2, CH, 9 * CH), bf16),
             mem((CH, 9 * CH), f32), mem((CH, 128), f32),
-            mem((16, 2, 8, 128), f32), mem((3, CH, 128), f32),
+            mem((16, 2, 8, 128), f32), mem((3, 8, 4, 128), f32),
             mem((16, 2, 8, 128), f32), mem((2, 8, 128), f32),
-            mem((16, 2, 8, 128), f32), mem((16, 2, 8, 128), f32), mem((24, CH, 128), f32),
-            dma((2,)), dma((6,)), dma((6,)), dma((8,)), dma((8,)),
+            mem((16, 2, 8, 128), f32), mem((24, 4, 128), f32),
+            dma((2,)), dma((6,)), dma((6,)), dma((8,)), dma((8,)), dma((8,)), dma((8,)),
             dma((16,)), dma((16,)), dma((16,)), dma((16,)), dma((16,)), dma((16,)),
-            dma((24,)), dma((24,)), dma,
+            dma((24,)), dma((24,)), dma((8,)), dma((8,)), dma,
         ],
-        compiler_params=pltpu.CompilerParams(collective_id=0, has_side_effects=True, vmem_limit_bytes=63 << 20),
+        compiler_params=pltpu.CompilerParams(collective_id=0, has_side_effects=True, vmem_limit_bytes=60 << 20),
         name="section",
     )(dilations, bin_embed, weights, biases, cotangent)
+    return pl.pallas_call(
+        finish,
+        out_shape=[shape((CH, TI, TK), bf16), shape((2, 9, CH, CH), f32), shape((2, CH), f32), shape((CH, TI), f32)],
+        in_specs=[hbm, vmem, vmem],
+        out_specs=[hbm, vmem, vmem, vmem],
+        scratch_shapes=[dma],
+        name="finish",
+    )(section, res, ge)
 
 
 def solution(mesh):

time: 91.5 us -> 110 us (1.20)
  Pallas kernels: 86.4 us -> 109 us
  local copies, waits for them, and re-layouts: 4.24 us -> 0 us
    pallas_call x1 -> x2, Pallas kernels: 86.4 us -> 109 us  [the longest x1 74.9 us: per_device(): pl.pallas_call(kernel, out_shape=[shape((CH, TI, TK), bf16), shape((16, 2...]
    unnamed x10 -> x0, local copies, waits for them, and re-layouts: 4.24 us -> none
where the time goes in v3:
time: 110 us
  Pallas kernels  109 us (99%)
    pallas_call x1, Pallas kernels, per_device(): pl.pallas_call(kernel, out_shape=[shape((CH, TI, TK), bf16), shape((16, 2...  74.9 us
    pallas_call x1, Pallas kernels, per_device(): pl.pallas_call(finish, out_shape=[shape((CH, TI, TK), bf16), shape((2, 9,...  34.5 us

profile of v3, /device:TPU:1, one launch (start us, length us, event | category | flops | bytes accessed | tf_op | source)
XLA Modules:
  0.0 110.0 jit_solution(10297298797188591637)
XLA Ops:
  0.6 74.9 %section.1 = (bf16[32,128,128]{2,1,0:T(8,128)(2,1)}, f32[16,2,8,128]{3,2,1,0:T(8,128)}, f32[8,4,128]{2,1,0:T(4,128)}) custom-call(s32[2]{0:T(128)} %dil.1, bf16[32,128]{1,0:T(8,128)(2,1)} %emb.1, bf16[2,9,32,32]{3,2,1,0:T(8,128)(2,1)} %w.1, f32[2,32]{1,0:T(2,128)} %bias.1, bf16[32,128,128]{2,1,0:T(8,128)(2,1)} %cot_hbm.1), custom_call_target="tpu_custom_call" | custom-call | tf_op jit(solution)/shard_map/section/pallas_call | solution.py:566
  75.5 34.5 %finish.1 = (bf16[32,128,128]{2,1,0:T(8,128)(2,1)}, f32[2,9,32,32]{3,2,1,0:T(8,128)}, f32[2,32]{1,0:T(2,128)}, f32[32,128]{1,0:T(8,128)}) custom-call(bf16[32,128,128]{2,1,0:T(8,128)(2,1)} %get-tuple-element.7.section, f32[16,2,8,128]{3,2,1,0:T(8,128)} %get-tuple-element.8.res, f32[8,4,128]{2,1,0:T(4,128)} %get-tuple-element.9.ge), custom_call_target="tpu_custom_call" | custom-call | tf_op jit(solution)/shard_map/finish/pallas_call | solution.py:589

commit v4 on v3

--- a/solution.py
+++ b/solution.py
@@ -22,9 +22,13 @@
     return lax.broadcasted_iota(jnp.int32, (CH, 128), 1)
 
 
-def in_range(amount):
-    p = lanes() + amount
-    return (p >= 0) & (p < 128)
+def level(value):
+    return jnp.full((CH, 128), value.astype(f32)).astype(bf16)
+
+
+def in_range(s, d):
+    p = lanes().astype(bf16)
+    return p < level(128 - s * d) if s > 0 else p >= level(-s * d)
 
 
 def turned(x, amount):
@@ -73,32 +77,65 @@
 
 def shift_tables(d):
     amounts = [s * d for s in (-2, -1, 0, 1, 2)]
-    return amounts, [in_range(t) for t in amounts]
-
-
-def phase_x0(row0, band0, d, ec, er, x0, s0, unroll=4):
-    amounts, insides = shift_tables(d)
+    return amounts, [in_range(s, d) for s in (-2, -1, 0, 1, 2)]
+
+
+LOW = -1e38
+
+
+def bounded_blocks(r, o, ec, er):
+    for n in range(1, 5):
+        ec[n] = jnp.where(r + o + n - 2 < NBINS // TI, ec[n], LOW)
+    for n in (0, 2):
+        ec_row = r + n - 1
+        er[n] = jnp.where((ec_row >= 0) & (ec_row < NBINS // TI), er[n], LOW)
+
+
+def lane_caps(band0, d, caps):
+    p = lanes()
+    for n, s in enumerate((-2, -1, 0, 1, 2)):
+        for half in range(2):
+            k = band0 + s * d + (jnp.where(p < 64, p + 128, p - 128) if half else p)
+            caps[2 * n + half] = jnp.where((k >= 0) & (k < KBAND), 3e38, 0.0).astype(bf16)
+
+
+def phase_windows(ec, win, unroll=32):
+    u = lanes()
+    ub = u.astype(bf16)
 
     def body(it, _):
+        m0 = it * unroll - 4 * DMAX
+        q = lax.div(m0 + 128, 128) - 1
+        t0 = m0 - 128 * q
+        prev, here, after, later = (ec[q + 1 + n] for n in range(4))
+        high = jnp.where((u >= 64) & (t0 < 32), prev, after)
+        low = jnp.where((u < 64) & (t0 >= 96), later, here)
+        for w in range(unroll):
+            t = t0 + w
+            beyond = ub >= level(t)
+            back = lax.rem(128 - t, 128)
+            win[it * unroll + w, :, 0:128] = pltpu.roll(jnp.where(beyond, here, after), back, 1)
+            win[it * unroll + w, :, 128:256] = pltpu.roll(jnp.where(beyond, high, low), back, 1)
+        return 0
+
+    lax.fori_loop(0, (H2 + 4 * DMAX) // unroll, body, 0)
+
+
+def phase_x0(d, er, win, caps, x0, s0, unroll=16):
+    def body(it, _):
+        i0 = it * unroll - 2 * DMAX
+        q = lax.div(i0 + 128, 128) - 1
+        block = pltpu.roll(er[q + 1], lax.rem(256 - (i0 - 128 * q), 128), 1)
         for w in range(unroll):
             j = it * unroll + w
-            i = j - 2 * DMAX
-            q = lax.div(i + 128, 128) - 1
-            t = i - q * 128
-            back = lax.rem(128 - t, 128)
-            re = [pltpu.roll(ec[q + 1 + n], back, 1) for n in range(4)]
-            cut = lanes() < 128 - t
-            wm = jnp.where(cut, re[0], re[1])
-            w0 = jnp.where(cut, re[1], re[2])
-            w1 = jnp.where(cut, re[2], re[3])
-            wb = jnp.where(lanes() < 64, w1, wm)
-            own = pltpu.roll(er[q + 1], back, 1).astype(f32)[:, 0:1]
-            ma, mb = row_masks(row0, band0, i)
-            a = jnp.where(ma, own + w0.astype(f32), 0.0).astype(bf16)
-            b = jnp.where(mb, own + wb.astype(f32), 0.0).astype(bf16)
-            x0[j, :, 0:128] = a
-            x0[j, :, 128:256] = b
-            store_shifts(s0, j, jnp.maximum(a, 0), jnp.maximum(b, 0), amounts, insides)
+            own = jnp.broadcast_to(block[:, w : w + 1], (CH, 128))
+            for n, s in enumerate((-2, -1, 0, 1, 2)):
+                for half in range(2):
+                    at = slice(128 * half, 128 * half + 128)
+                    v = own + win[j + 2 * DMAX + s * d, :, at]
+                    if s == 0:
+                        x0[j, :, at] = v
+                    s0[j, CH * n : CH * n + CH, at] = jnp.minimum(jnp.maximum(v, 0), caps[2 * n + half])
         return 0
 
     lax.fori_loop(0, H2 // unroll, body, 0)
@@ -146,7 +183,7 @@
     lax.fori_loop(0, TI // unroll, body, 0)
 
 
-def phase_gw(h, s, soff, d, gw, gb, unroll=16):
+def phase_gw(h, s, soff, d, gw, gb, unroll=64):
     def body(it, carry):
         acc, accb = carry
         for w in range(0, unroll, 2):
@@ -177,9 +214,9 @@
     return left, right
 
 
-def phase_shift(row0, band0, d, rows, rl, rr, dst, unroll=2):
+def phase_shift(row0, band0, d, rows, rl, rr, dst, unroll=3):
     lane = lanes()
-    insides = [in_range(s * d) for s in (-2, -1, 1, 2)]
+    insides = [in_range(s, d) for s in (-2, -1, 1, 2)]
 
     def body(it, _):
         for g in range(unroll):
@@ -209,7 +246,7 @@
     lax.fori_loop(0, H1 // 8 // unroll, body, 0)
 
 
-def phase_g1(d, wb, x1, t1, ga, gpl, gpr, unroll=16):
+def phase_g1(d, wb, x1, t1, ga, gpl, gpr, unroll=64):
     def body(it, _):
         rows = []
         for w in range(0, unroll, 2):
@@ -231,11 +268,13 @@
     lax.fori_loop(0, TI // unroll, body, 0)
 
 
-def phase_g0(d, wb, x0, t0, unroll=4):
+def phase_g0(d, wb, s0, t0, unroll=32):
     lane = lanes()
+    ones = jnp.ones((128, 128), bf16)
 
     def body(it, carry):
         rsum, lo, hi = carry
+        rows = []
         for w in range(0, unroll, 2):
             i = it * unroll + w
             j = i + DMAX
@@ -243,14 +282,16 @@
             q = jnp.dot(wb, x, preferred_element_type=f32)
             for z in range(2):
                 g1 = t0[j + z, 64:96, 0:128].astype(f32)
-                gate = x0[j + z + DMAX, :, 0:128].astype(f32) > 0
+                gate = s0[j + z + DMAX, 64:96, 0:128].astype(f32) > 0
                 gp = (g1 + jnp.where(gate, q[:, 128 * z : 128 * z + 128], 0.0)).astype(bf16)
-                gf = gp.astype(f32)
-                rsum = jnp.where(lane == i + z, jnp.sum(gf, axis=1, keepdims=True), rsum)
+                rows.append(gp)
                 moved = pltpu.roll(gp, i + z, 1).astype(f32)
                 low = jnp.where(lane >= i + z, moved, 0.0)
                 lo = lo + low
                 hi = hi + (moved - low)
+        sums = jnp.dot(jnp.concatenate(rows, axis=0), ones, preferred_element_type=f32)
+        for w in range(unroll):
+            rsum = jnp.where(lane == it * unroll + w, sums[CH * w : CH * w + CH], rsum)
         return rsum, lo, hi
 
     zero = jnp.zeros((CH, 128), f32)
@@ -360,7 +401,7 @@
 def kernel(
     dil, emb, w, bias, cot_hbm, out_hbm, res, ge,
     cot, out, ec, er, a, rl, rr, pl_, pr_, ga, grl, grr, gpl, gpr, x0, x1, s0, t1, s1, t0, wf, wb, gw, gb,
-    pay, terms, wr1, w2, wr2, inbox,
+    pay, terms, wr1, w2, wr2, inbox, win, caps,
     io, esend, erecv, hsend, hrecv, gsend, grecv, sa, ra, sb, rb, sc, rc, st, rt, su, ru, local_sem,
 ):
     r, o = lax.axis_index("diag"), lax.axis_index("off")
@@ -401,7 +442,9 @@
     ec[0] = jnp.zeros((CH, 128), bf16)
     ec[5] = jnp.zeros((CH, 128), bf16)
     er[1] = emb[...]
+    d0, d1 = dil[0], dil[1]
     place_weights(w, wf, wb)
+    lane_caps(band0, d0, caps)
     fetch.wait()
     lay_rows(cot, a, pl_, pr_)
     pl.semaphore_wait(barrier, count)
@@ -415,11 +458,12 @@
     def column(layer):
         return jnp.sum(jnp.where(eye, bias[layer : layer + 1, :], 0.0), axis=1, keepdims=True)
 
-    d0, d1 = dil[0], dil[1]
     for c in ecopies:
         c.wait_recv()
-    phase_x0(row0, band0, d0, ec, er, x0, s0, 8)
-    phase_x1(row0, band0, d0, d1, wf[0], column(0), x0, s0, x1, s1, 16)
+    bounded_blocks(r, o, ec, er)
+    phase_windows(ec, win)
+    phase_x0(d0, er, win, caps, x0, s0)
+    phase_x1(row0, band0, d0, d1, wf[0], column(0), x0, s0, x1, s1, 48)
     for c in hcopies:
         c.wait_recv()
     phase_shift(row0, band0, d1, a, rl, rr, t1)
@@ -443,7 +487,7 @@
     for c in gcopies:
         c.wait_recv()
     phase_shift(row0, band0, d0, ga, grl, grr, t0)
-    rsum, lo, hi = phase_g0(d0, wb[0], x0, t0, 16)
+    rsum, lo, hi = phase_g0(d0, wb[0], s0, t0)
     for n in range(8):
         rows = slice(4 * n, 4 * n + 4)
         terms[0, n] = rsum[rows]
@@ -491,7 +535,7 @@
     for c in second:
         c.start()
 
-    phase_x2(row0, band0, d1, wf[1], column(1), x1, s1, out, 32)
+    phase_x2(row0, band0, d1, wf[1], column(1), x1, s1, out, 64)
     write = pltpu.make_async_copy(out, out_hbm, io.at[1])
     write.start()
 
@@ -545,13 +589,14 @@
     write.wait()
 
 
-def finish(section, res, ge, out, gw_out, gb_out, ge_out, sem):
-    move = pltpu.make_async_copy(section, out, sem)
-    move.start()
-    unpack_grads(res, gw_out, gb_out)
-    for n in range(8):
-        ge_out[4 * n : 4 * n + 4, :] = ge[n]
-    move.wait()
+def finish(section, res, ge, out, gw_out, gb_out, ge_out):
+    out[...] = section[...]
+
+    @pl.when(pl.program_id(0) == 0)
+    def _():
+        unpack_grads(res, gw_out, gb_out)
+        for n in range(8):
+            ge_out[4 * n : 4 * n + 4, :] = ge[n]
 
 
 def per_device(bin_embed, weights, biases, dilations, cotangent):
@@ -579,6 +624,7 @@
             mem((16, 2, 8, 128), f32), mem((3, 8, 4, 128), f32),
             mem((16, 2, 8, 128), f32), mem((2, 8, 128), f32),
             mem((16, 2, 8, 128), f32), mem((24, 4, 128), f32),
+            mem((H2 + 4 * DMAX, CH, 256), bf16), mem((10, CH, 128), bf16),
             dma((2,)), dma((6,)), dma((6,)), dma((8,)), dma((8,)), dma((8,)), dma((8,)),
             dma((16,)), dma((16,)), dma((16,)), dma((16,)), dma((16,)), dma((16,)),
             dma((24,)), dma((24,)), dma((8,)), dma((8,)), dma,
@@ -586,12 +632,13 @@
         compiler_params=pltpu.CompilerParams(collective_id=0, has_side_effects=True, vmem_limit_bytes=60 << 20),
         name="section",
     )(dilations, bin_embed, weights, biases, cotangent)
+    part = pl.BlockSpec((8, TI, TK), lambda n: (n, 0, 0))
     return pl.pallas_call(
         finish,
+        grid=(CH // 8,),
         out_shape=[shape((CH, TI, TK), bf16), shape((2, 9, CH, CH), f32), shape((2, CH), f32), shape((CH, TI), f32)],
-        in_specs=[hbm, vmem, vmem],
-        out_specs=[hbm, vmem, vmem, vmem],
-        scratch_shapes=[dma],
+        in_specs=[part, vmem, vmem],
+        out_specs=[part, vmem, vmem, vmem],
         name="finish",
     )(section, res, ge)
 

time: 110 us -> 69.5 us (0.63)
  Pallas kernels: 109 us -> 68.7 us
    pallas_call x1, Pallas kernels: 34.5 us -> 3.65 us  [per_device(): pl.pallas_call(finish, grid=(CH // 8,), out_shape=[shape((CH, TI, TK), bf...]
    pallas_call x1, Pallas kernels: 74.9 us -> 65 us  [per_device(): pl.pallas_call(kernel, out_shape=[shape((CH, TI, TK), bf16), shape((16, 2...]
where the time goes in v4:
time: 69.5 us; the launch traced here: 69.3 us
  Pallas kernels  68.7 us (99%)
    pallas_call x1, Pallas kernels, per_device(): pl.pallas_call(kernel, out_shape=[shape((CH, TI, TK), bf16), shape((16, 2...  65 us
    pallas_call x1, Pallas kernels, per_device(): pl.pallas_call(finish, grid=(CH // 8,), out_shape=[shape((CH, TI, TK), bf...  3.65 us

profile of v4, /device:TPU:1, one launch (start us, length us, event | category | flops | bytes accessed | tf_op | source)
XLA Modules:
  0.0 69.3 jit_solution(1292845629068215594)
XLA Ops:
  0.6 65.0 %section.1 = (bf16[32,128,128]{2,1,0:T(8,128)(2,1)}, f32[16,2,8,128]{3,2,1,0:T(8,128)}, f32[8,4,128]{2,1,0:T(4,128)}) custom-call(s32[2]{0:T(128)} %dil.1, bf16[32,128]{1,0:T(8,128)(2,1)} %emb.1, bf16[2,9,32,32]{3,2,1,0:T(8,128)(2,1)} %w.1, f32[2,32]{1,0:T(2,128)} %bias.1, bf16[32,128,128]{2,1,0:T(8,128)(2,1)} %cot_hbm.1), custom_call_target="tpu_custom_call" | custom-call | tf_op jit(solution)/shard_map/section/pallas_call | solution.py:611
  65.7 3.7 %finish.1 = (bf16[32,128,128]{2,1,0:T(8,128)(2,1)}, f32[2,9,32,32]{3,2,1,0:T(8,128)}, f32[2,32]{1,0:T(2,128)}, f32[32,128]{1,0:T(8,128)}) custom-call(bf16[32,128,128]{2,1,0:T(8,128)(2,1)} %get-tuple-element.7.section, f32[16,2,8,128]{3,2,1,0:T(8,128)} %get-tuple-element.8.res, f32[8,4,128]{2,1,0:T(4,128)} %get-tuple-element.9.ge), custom_call_target="tpu_custom_call" | custom-call | tf_op jit(solution)/shard_map/finish/pallas_call | solution.py:636

commit v5 on v4

--- a/solution.py
+++ b/solution.py
@@ -214,14 +214,14 @@
     return left, right
 
 
-def phase_shift(row0, band0, d, rows, rl, rr, dst, unroll=3):
+def phase_shift(row0, band0, d, depth, rows, rl, rr, dst, unroll):
     lane = lanes()
     insides = [in_range(s, d) for s in (-2, -1, 1, 2)]
 
     def body(it, _):
         for g in range(unroll):
             group = it * unroll + g
-            first = row0 + group * 8 - DMAX
+            first = row0 + group * 8 - depth
             row = first + lax.div(lane, 16)
             kr = band0 + 128 + lax.rem(lane, 16)
             kl = band0 - 16 + lax.rem(lane, 16)
@@ -243,18 +243,18 @@
                     )
         return 0
 
-    lax.fori_loop(0, H1 // 8 // unroll, body, 0)
-
-
-def phase_g1(d, wb, x1, t1, ga, gpl, gpr, unroll=64):
+    lax.fori_loop(0, (TI + 2 * depth) // 8 // unroll, body, 0)
+
+
+def phase_g1(d, wb, x1, t1, ga, gpl, gpr, unroll=48):
     def body(it, _):
         rows = []
         for w in range(0, unroll, 2):
-            j = it * unroll + w + DMAX
-            x = jnp.concatenate([taps(t1, j, d, 0, 128), taps(t1, j + 1, d, 0, 128)], axis=1)
+            j = it * unroll + w
+            x = jnp.concatenate([taps(t1, j + DMAX, d, 0, 128), taps(t1, j + DMAX + 1, d, 0, 128)], axis=1)
             q = jnp.dot(wb, x, preferred_element_type=f32)
             for z in range(2):
-                h = t1[j + z, 64:96, :].astype(f32)
+                h = t1[j + DMAX + z, 64:96, :].astype(f32)
                 gate = x1[j + z, :, 0:128].astype(f32) > 0
                 g = (h + jnp.where(gate, q[:, 128 * z : 128 * z + 128], 0.0)).astype(bf16)
                 ga[j + z] = g
@@ -265,10 +265,10 @@
             gpr[it * (unroll // 8) + n] = right
         return 0
 
-    lax.fori_loop(0, TI // unroll, body, 0)
-
-
-def phase_g0(d, wb, s0, t0, unroll=32):
+    lax.fori_loop(0, H1 // unroll, body, 0)
+
+
+def phase_g0(d, wb, s0, t0, begin, end, carry, unroll=32):
     lane = lanes()
     ones = jnp.ones((128, 128), bf16)
 
@@ -294,8 +294,7 @@
             rsum = jnp.where(lane == it * unroll + w, sums[CH * w : CH * w + CH], rsum)
         return rsum, lo, hi
 
-    zero = jnp.zeros((CH, 128), f32)
-    return lax.fori_loop(0, TI // unroll, body, (zero, zero, zero))
+    return lax.fori_loop(begin // unroll, end // unroll, body, carry)
 MESH = pl.DeviceIdType.MESH
 NR, NO = 32, 8
 
@@ -350,14 +349,14 @@
 
 def halo_copies(r, o, a, pl_, pr_, rl, rr, send, recv):
     jobs = [
-        (pl_, rl.at[1:17], 0, -1),
-        (pr_, rr.at[1:17], 0, 1),
-        (a.at[128:136], a.at[0:8], 1, 0),
-        (a.at[8:16], a.at[136:144], -1, 0),
-        (pl_.at[15:16], rl.at[0:1], 1, -1),
-        (pl_.at[0:1], rl.at[17:18], -1, -1),
-        (pr_.at[15:16], rr.at[0:1], 1, 1),
-        (pr_.at[0:1], rr.at[17:18], -1, 1),
+        (pl_, rl.at[2:18], 0, -1),
+        (pr_, rr.at[2:18], 0, 1),
+        (a.at[128:144], a.at[0:16], 1, 0),
+        (a.at[16:32], a.at[144:160], -1, 0),
+        (pl_.at[14:16], rl.at[0:2], 1, -1),
+        (pl_.at[0:2], rl.at[18:20], -1, -1),
+        (pr_.at[14:16], rr.at[0:2], 1, 1),
+        (pr_.at[0:2], rr.at[18:20], -1, 1),
     ]
     return [
         remote(src, dst, send.at[n], recv.at[n], wrap(r + dr, o + do))
@@ -388,7 +387,7 @@
 def lay_rows(cot, a, pl_, pr_):
     def body(it, _):
         block = jnp.swapaxes(cot[:, pl.ds(pl.multiple_of(it * 16, 16), 16), :], 0, 1)
-        a[pl.ds(DMAX + it * 16, 16)] = block
+        a[pl.ds(2 * DMAX + it * 16, 16)] = block
         for n in range(2):
             left, right = packed([block[8 * n + w] for w in range(8)])
             pl_[it * 2 + n] = left
@@ -399,17 +398,21 @@
 
 
 def kernel(
-    dil, emb, w, bias, cot_hbm, out_hbm, res, ge,
-    cot, out, ec, er, a, rl, rr, pl_, pr_, ga, grl, grr, gpl, gpr, x0, x1, s0, t1, s1, t0, wf, wb, gw, gb,
-    pay, terms, wr1, w2, wr2, inbox, win, caps,
+    dil, emb_hbm, w_hbm, bias_hbm, cot_hbm, out_hbm, res, ge,
+    emb, w, bias, cot, out, ec, er, a, rl, rr, pl_, pr_, ga, grl, grr, gpl, gpr, x0, x1, s0, t1, s1, t0, wf, wb, gw, gb,
+    pay, terms, wr1, w2, wr2, inbox, shares, win, caps,
     io, esend, erecv, hsend, hrecv, gsend, grecv, sa, ra, sb, rb, sc, rc, st, rt, su, ru, local_sem,
 ):
     r, o = lax.axis_index("diag"), lax.axis_index("off")
     core, b = lax.rem(r, 2), lax.div(r, 2)
     me = o * 2 + core
     row0, band0 = r * TI, o * TK
-    fetch = pltpu.make_async_copy(cot_hbm, cot, io.at[0])
-    fetch.start()
+    fetches = [
+        pltpu.make_async_copy(src, dst, io.at[n])
+        for n, (src, dst) in enumerate(((emb_hbm, emb), (w_hbm, w), (bias_hbm, bias), (cot_hbm, cot)))
+    ]
+    for c in fetches:
+        c.start()
 
     def peer_a(n):
         other = lax.rem(me + n, 16)
@@ -428,24 +431,21 @@
     for n in range(1, 16):
         greet(peer_a(n)[1])
         greet(peer_b(n)[1])
-    for n in range(1, 8):
-        oo = lax.rem(o + n, 8)
-        greet(wrap(r - oo, oo))
-        greet(wrap(r - oo - 1, oo))
     greet(wrap(r - o - 1, o))
 
     @pl.when(o > 0)
     def _():
         greet(wrap(r - o, o))
 
-    count = count + 30 + 14 + 1 + jnp.minimum(o, 1)
+    count = count + 30 + 1 + jnp.minimum(o, 1)
     ec[0] = jnp.zeros((CH, 128), bf16)
     ec[5] = jnp.zeros((CH, 128), bf16)
+    d0, d1 = dil[0], dil[1]
+    lane_caps(band0, d0, caps)
+    for c in fetches:
+        c.wait()
     er[1] = emb[...]
-    d0, d1 = dil[0], dil[1]
     place_weights(w, wf, wb)
-    lane_caps(band0, d0, caps)
-    fetch.wait()
     lay_rows(cot, a, pl_, pr_)
     pl.semaphore_wait(barrier, count)
     ecopies = embed_copies(r, o, emb, ec, er, esend, erecv)
@@ -466,12 +466,15 @@
     phase_x1(row0, band0, d0, d1, wf[0], column(0), x0, s0, x1, s1, 48)
     for c in hcopies:
         c.wait_recv()
-    phase_shift(row0, band0, d1, a, rl, rr, t1)
+    phase_shift(row0, band0, d1, 2 * DMAX, a, rl, rr, t1, 4)
     phase_g1(d1, wb[1], x1, t1, ga, gpl, gpr)
-    gcopies = halo_copies(r, o, ga, gpl, gpr, grl, grr, gsend, grecv)
+    gcopies = [
+        remote(gpl, grl, gsend.at[0], grecv.at[0], wrap(r, o - 1)),
+        remote(gpr, grr, gsend.at[1], grecv.at[1], wrap(r, o + 1)),
+    ]
     for c in gcopies:
         c.start()
-    phase_gw(lambda i: t1[i + DMAX, 64:96, :], s1, DMAX, d1, gw, gb)
+    phase_gw(lambda i: t1[i + 2 * DMAX, 64:96, :], s1, DMAX, d1, gw, gb)
     third1 = pack_grads(1, gw, gb, pay)
     phase_gw(lambda i: ga[i + DMAX], s0, 2 * DMAX, d0, gw, gb)
     third0 = pack_grads(0, gw, gb, pay)
@@ -486,36 +489,7 @@
 
     for c in gcopies:
         c.wait_recv()
-    phase_shift(row0, band0, d0, ga, grl, grr, t0)
-    rsum, lo, hi = phase_g0(d0, wb[0], s0, t0)
-    for n in range(8):
-        rows = slice(4 * n, 4 * n + 4)
-        terms[0, n] = rsum[rows]
-        terms[1, n] = lo[rows]
-        terms[2, n] = hi[rows]
-    eout = []
-    for n in range(0, 8):
-        oo = lax.rem(o + n, 8)
-        for kind, dr in ((0, 0), (1, o), (2, o + 1)):
-            if n == 0 and kind < 2:
-                continue
-            eout.append(remote(terms.at[kind, oo], inbox.at[kind * 8 + o], st.at[kind * 8 + n], rt.at[kind * 8 + o], wrap(r + dr, oo)))
-    for c in eout:
-        c.start()
-    own = remote(terms.at[1, o], inbox.at[8 + o], st.at[8], rt.at[8 + o], wrap(r + o, o))
-
-    @pl.when(o > 0)
-    def _():
-        own.start()
-
-    local = pltpu.make_async_copy(terms.at[1, o], inbox.at[8 + o], local_sem)
-
-    @pl.when(o == 0)
-    def _():
-        local.start()
-
-    inbox[o] = terms[0, o]
-
+    phase_shift(row0, band0, d0, DMAX, ga, grl, grr, t0, 3)
     def arrived(dst, sem):
         pltpu.make_async_copy(dst, dst, sem).wait()
 
@@ -525,6 +499,8 @@
             acc = acc + buf[n]
         return acc
 
+    zero = jnp.zeros((CH, TI), f32)
+    sums = phase_g0(d0, wb[0], s0, t0, 0, 64, (zero, zero, zero))
     wr1[me] = pay[me]
     for n in range(1, 16):
         other, _t = peer_a(n)
@@ -535,32 +511,37 @@
     for c in second:
         c.start()
 
+    rsum, lo, hi = phase_g0(d0, wb[0], s0, t0, 64, 128, sums)
+    terms[0] = lo
+    terms[1] = hi
+    low = remote(terms.at[0], inbox.at[0], st.at[0], rt.at[0], wrap(r + o, o))
+    high = remote(terms.at[1], inbox.at[1], st.at[1], rt.at[1], wrap(r + o + 1, o))
+    high.start()
+    local = pltpu.make_async_copy(terms.at[0], inbox.at[0], local_sem)
+
+    @pl.when(o > 0)
+    def _():
+        low.start()
+
+    @pl.when(o == 0)
+    def _():
+        local.start()
+
     phase_x2(row0, band0, d1, wf[1], column(1), x1, s1, out, 64)
-    write = pltpu.make_async_copy(out, out_hbm, io.at[1])
+    write = pltpu.make_async_copy(out, out_hbm, io.at[4])
     write.start()
 
-    for kind in range(3):
-        for n in range(8):
-            if kind == 0 and n == 0:
-                continue
-            oo = lax.rem(o + n, 8)
-            slot = kind * 8 + oo
-            if kind == 1 and n == 0:
-                @pl.when(o > 0)
-                def _():
-                    arrived(inbox.at[slot], rt.at[slot])
-            else:
-                arrived(inbox.at[slot], rt.at[slot])
+    @pl.when(o > 0)
+    def _():
+        low.wait_recv()
 
     @pl.when(o == 0)
     def _():
         local.wait()
 
-    acc = inbox[0]
-    for n in range(1, 24):
-        acc = acc + inbox[n]
-    ge[o] = acc
-    eall = [remote(ge.at[o], ge.at[o], su.at[n], ru.at[o], wrap(r, o + n)) for n in range(1, 8)]
+    high.wait_recv()
+    shares[o] = rsum + inbox[0] + inbox[1]
+    eall = [remote(shares.at[o], shares.at[o], su.at[n], ru.at[o], wrap(r, o + n)) for n in range(1, 8)]
     for c in eall:
         c.start()
 
@@ -575,28 +556,38 @@
         c.start()
     for n in range(1, 8):
         oo = lax.rem(o + n, 8)
-        arrived(ge.at[oo], ru.at[oo])
+        arrived(shares.at[oo], ru.at[oo])
+    acc = shares[0]
+    for n in range(1, 8):
+        acc = acc + shares[n]
+    ge[...] = acc
     for n in range(1, 16):
         other, _t = peer_a(n)
         arrived(res.at[other], rc.at[other])
-    for c in first + second + third + eout + eall + ecopies + hcopies + gcopies:
+    for c in first + second + third + [high] + eall + ecopies + hcopies + gcopies:
         c.wait_send()
 
     @pl.when(o > 0)
     def _():
-        own.wait_send()
+        low.wait_send()
 
     write.wait()
 
 
-def finish(section, res, ge, out, gw_out, gb_out, ge_out):
-    out[...] = section[...]
-
-    @pl.when(pl.program_id(0) == 0)
-    def _():
-        unpack_grads(res, gw_out, gb_out)
-        for n in range(8):
-            ge_out[4 * n : 4 * n + 4, :] = ge[n]
+def finish(section, res, ge, out, gw_out, gb_out, ge_out, held, come, go):
+    size = CH // 4
+    parts = [slice(n * size, n * size + size) for n in range(4)]
+    ins = [pltpu.make_async_copy(section.at[p], held.at[p], come.at[n]) for n, p in enumerate(parts)]
+    outs = [pltpu.make_async_copy(held.at[p], out.at[p], go.at[n]) for n, p in enumerate(parts)]
+    for c in ins:
+        c.start()
+    for n in range(4):
+        ins[n].wait()
+        outs[n].start()
+    unpack_grads(res, gw_out, gb_out)
+    ge_out[...] = ge[...]
+    for c in outs:
+        c.wait()
 
 
 def per_device(bin_embed, weights, biases, dilations, cotangent):
@@ -606,41 +597,43 @@
     shape = jax.ShapeDtypeStruct
     dma = pltpu.SemaphoreType.DMA
     mem = pltpu.VMEM
-    halo = [mem((H1, CH, 128), bf16), mem((18, CH, 128), bf16), mem((18, CH, 128), bf16),
+    halo = [mem((H2, CH, 128), bf16), mem((20, CH, 128), bf16), mem((20, CH, 128), bf16),
             mem((16, CH, 128), bf16), mem((16, CH, 128), bf16)]
+    edge = [mem((H1, CH, 128), bf16)] + [mem((18, CH, 128), bf16)] * 4
     section, res, ge = pl.pallas_call(
         kernel,
-        out_shape=[shape((CH, TI, TK), bf16), shape((16, 2, 8, 128), f32), shape((8, 4, 128), f32)],
-        in_specs=[smem, vmem, vmem, vmem, hbm],
+        out_shape=[shape((CH, TI, TK), bf16), shape((16, 2, 8, 128), f32), shape((CH, TI), f32)],
+        in_specs=[smem, hbm, hbm, hbm, hbm],
         out_specs=[hbm, vmem, vmem],
         scratch_shapes=[
+            mem((CH, TI), bf16), mem((2, 9, CH, CH), bf16), mem((2, CH), f32),
             mem((CH, TI, TK), bf16), mem((CH, TI, TK), bf16),
-            mem((6, CH, 128), bf16), mem((3, CH, 128), bf16), *halo, *halo,
+            mem((6, CH, 128), bf16), mem((3, CH, 128), bf16), *halo, *edge,
             mem((H2, CH, 256), bf16), mem((H1, CH, 256), bf16),
-            mem((H2, 5 * CH, 256), bf16), mem((H1, 5 * CH, 128), bf16),
+            mem((H2, 5 * CH, 256), bf16), mem((H2, 5 * CH, 128), bf16),
             mem((H1, 5 * CH, 128), bf16), mem((H1, 5 * CH, 128), bf16),
             mem((2, CH, 9 * CH), bf16), mem((2, CH, 9 * CH), bf16),
             mem((CH, 9 * CH), f32), mem((CH, 128), f32),
-            mem((16, 2, 8, 128), f32), mem((3, 8, 4, 128), f32),
+            mem((16, 2, 8, 128), f32), mem((2, CH, TI), f32),
             mem((16, 2, 8, 128), f32), mem((2, 8, 128), f32),
-            mem((16, 2, 8, 128), f32), mem((24, 4, 128), f32),
+            mem((16, 2, 8, 128), f32), mem((2, CH, TI), f32), mem((8, CH, TI), f32),
             mem((H2 + 4 * DMAX, CH, 256), bf16), mem((10, CH, 128), bf16),
-            dma((2,)), dma((6,)), dma((6,)), dma((8,)), dma((8,)), dma((8,)), dma((8,)),
+            dma((5,)), dma((6,)), dma((6,)), dma((8,)), dma((8,)), dma((2,)), dma((2,)),
             dma((16,)), dma((16,)), dma((16,)), dma((16,)), dma((16,)), dma((16,)),
-            dma((24,)), dma((24,)), dma((8,)), dma((8,)), dma,
+            dma((2,)), dma((2,)), dma((8,)), dma((8,)), dma,
         ],
         compiler_params=pltpu.CompilerParams(collective_id=0, has_side_effects=True, vmem_limit_bytes=60 << 20),
         name="section",
     )(dilations, bin_embed, weights, biases, cotangent)
-    part = pl.BlockSpec((8, TI, TK), lambda n: (n, 0, 0))
-    return pl.pallas_call(
+    out, gw, gb, ge_out = pl.pallas_call(
         finish,
-        grid=(CH // 8,),
         out_shape=[shape((CH, TI, TK), bf16), shape((2, 9, CH, CH), f32), shape((2, CH), f32), shape((CH, TI), f32)],
-        in_specs=[part, vmem, vmem],
-        out_specs=[part, vmem, vmem, vmem],
+        in_specs=[hbm, vmem, vmem],
+        out_specs=[hbm, vmem, vmem, vmem],
+        scratch_shapes=[mem((CH, TI, TK), bf16), dma((4,)), dma((4,))],
         name="finish",
     )(section, res, ge)
+    return out, gw, gb, ge_out
 
 
 def solution(mesh):

time: 69.5 us -> 66.6 us (0.958)
  Pallas kernels: 68.7 us -> 65.8 us
    pallas_call x1, Pallas kernels: 65 us -> 62.2 us  [per_device(): pl.pallas_call(kernel, out_shape=[shape((CH, TI, TK), bf16), shape((16, 2...]
where the time goes in v5:
time: 66.6 us; the launch traced here: 66.4 us
  Pallas kernels  65.8 us (99%)
    pallas_call x1, Pallas kernels, per_device(): pl.pallas_call(kernel, out_shape=[shape((CH, TI, TK), bf16), shape((16, 2...  62.2 us
    pallas_call x1, Pallas kernels, per_device(): pl.pallas_call(finish, out_shape=[shape((CH, TI, TK), bf16), shape((2, 9,...  3.61 us

profile of v5, /device:TPU:1, one launch (start us, length us, event | category | flops | bytes accessed | tf_op | source)
XLA Modules:
  0.0 66.4 jit_solution(2465787442021165951)
XLA Ops:
  0.6 62.2 %section.1 = (bf16[32,128,128]{2,1,0:T(8,128)(2,1)}, f32[16,2,8,128]{3,2,1,0:T(8,128)}, f32[32,128]{1,0:T(8,128)}) custom-call(s32[2]{0:T(128)} %dil.1, bf16[32,128]{1,0:T(8,128)(2,1)} %emb_hbm.1, bf16[2,9,32,32]{3,2,1,0:T(8,128)(2,1)} %w_hbm.1, f32[2,32]{1,0:T(2,128)} %bias_hbm.1, bf16[32,128,128]{2,1,0:T(8,128)(2,1)} %cot_hbm.1), custom_call_target="tpu_custom_call" | custom-call | tf_op jit(solution)/shard_map/section/pallas_call | solution.py:603
  62.8 3.6 %finish.1 = (bf16[32,128,128]{2,1,0:T(8,128)(2,1)}, f32[2,9,32,32]{3,2,1,0:T(8,128)}, f32[2,32]{1,0:T(2,128)}, f32[32,128]{1,0:T(8,128)}) custom-call(bf16[32,128,128]{2,1,0:T(8,128)(2,1)} %get-tuple-element.7.section, f32[16,2,8,128]{3,2,1,0:T(8,128)} %get-tuple-element.8.res, f32[32,128]{1,0:T(8,128)} %get-tuple-element.9.ge), custom_call_target="tpu_custom_call" | custom-call | tf_op jit(solution)/shard_map/finish/pallas_call | solution.py:628

commit v6 on v5

--- a/solution.py
+++ b/solution.py
@@ -214,39 +214,88 @@
     return left, right
 
 
-def phase_shift(row0, band0, d, depth, rows, rl, rr, dst, unroll):
+SHIFTS = ((0, -2), (1, -1), (3, 1), (4, 2))
+
+
+def block_of(n):
+    return slice(CH * n, CH * n + CH)
+
+
+def rolled(x, s, d):
+    return pltpu.roll(x, lax.rem(256 - s * d, 128), 1)
+
+
+def halo_sides(row0, band0, depth, group, rl, rr):
     lane = lanes()
-    insides = [in_range(s, d) for s in (-2, -1, 1, 2)]
+    row = row0 + group * 8 - depth + lax.div(lane, 16)
+    kr = band0 + 128 + lax.rem(lane, 16)
+    kl = band0 - 16 + lax.rem(lane, 16)
+    right = jnp.where((row >= 0) & (kr < KBAND) & (kr < NBINS - row), rl[group], 0)
+    left = jnp.where((row >= 0) & (kl >= 0) & (kl < NBINS - row), rr[group], 0)
+    return right, left
+
+
+def side_of(right, left, w, s, d):
+    if s > 0:
+        return pltpu.roll(right, lax.rem(256 - 16 * w - s * d, 128), 1)
+    return pltpu.roll(left, lax.rem(256 + 16 * (7 - w) - s * d, 128), 1)
+
+
+def put_row(row0, band0, d, depth, j, a, dst):
+    row = row0 + j - depth
+    live = (row >= 0) & (band0 + lanes() < NBINS - row)
+    a = jnp.where(live, a, 0)
+    dst[j, block_of(2), :] = a
+    for m, s in SHIFTS:
+        dst[j, block_of(m), :] = rolled(a, s, d)
+
+
+def patch_group(row0, band0, d, depth, group, insides, rl, rr, dst):
+    right, left = halo_sides(row0, band0, depth, group, rl, rr)
+    for w in range(8):
+        j = group * 8 + w
+        for n, (m, s) in enumerate(SHIFTS):
+            dst[j, block_of(m), :] = jnp.where(
+                insides[n], dst[j, block_of(m), :], side_of(right, left, w, s, d)
+            )
+
+
+def inside_masks(d):
+    return [in_range(s, d) for _m, s in SHIFTS]
+
+
+def phase_patch(row0, band0, d, depth, groups, rl, rr, dst, unroll):
+    insides = inside_masks(d)
 
     def body(it, _):
         for g in range(unroll):
-            group = it * unroll + g
-            first = row0 + group * 8 - depth
-            row = first + lax.div(lane, 16)
-            kr = band0 + 128 + lax.rem(lane, 16)
-            kl = band0 - 16 + lax.rem(lane, 16)
-            right = jnp.where((row >= 0) & (kr < KBAND) & (kr < NBINS - row), rl[group], 0)
-            left = jnp.where((row >= 0) & (kl >= 0) & (kl < NBINS - row), rr[group], 0)
-            for w in range(8):
-                j = group * 8 + w
-                live = (first + w >= 0) & (band0 + lane < NBINS - (first + w))
-                a = jnp.where(live, rows[j], 0)
-                dst[j, 64:96, :] = a
-                for n, s in enumerate((-2, -1, 1, 2)):
-                    if s > 0:
-                        side = pltpu.roll(right, lax.rem(256 - 16 * w - s * d, 128), 1)
-                    else:
-                        side = pltpu.roll(left, lax.rem(256 + 16 * (7 - w) - s * d, 128), 1)
-                    m = n if s < 0 else n + 1
-                    dst[j, CH * m : CH * m + CH, :] = jnp.where(
-                        insides[n], pltpu.roll(a, lax.rem(256 - s * d, 128), 1), side
-                    )
-        return 0
-
-    lax.fori_loop(0, (TI + 2 * depth) // 8 // unroll, body, 0)
-
-
-def phase_g1(d, wb, x1, t1, ga, gpl, gpr, unroll=48):
+            patch_group(row0, band0, d, depth, it * unroll + g, insides, rl, rr, dst)
+        return 0
+
+    lax.fori_loop(0, groups // unroll, body, 0)
+
+
+def phase_own_shifts(row0, band0, d, a, dst, unroll=32):
+    def body(it, _):
+        for w in range(unroll):
+            j = 2 * DMAX + it * unroll + w
+            put_row(row0, band0, d, 2 * DMAX, j, a[j], dst)
+        return 0
+
+    lax.fori_loop(0, TI // unroll, body, 0)
+
+
+def phase_rim_shifts(row0, band0, d, a, dst):
+    def body(it, _):
+        for w in range(16):
+            j = it * 144 + w
+            put_row(row0, band0, d, 2 * DMAX, j, a[j], dst)
+        return 0
+
+    lax.fori_loop(0, 2, body, 0)
+
+
+def phase_g1(d, dn, wb, x1, t1, t0, gpl, gpr, send_chunk, unroll=48):
     def body(it, _):
         rows = []
         for w in range(0, unroll, 2):
@@ -257,12 +306,17 @@
                 h = t1[j + DMAX + z, 64:96, :].astype(f32)
                 gate = x1[j + z, :, 0:128].astype(f32) > 0
                 g = (h + jnp.where(gate, q[:, 128 * z : 128 * z + 128], 0.0)).astype(bf16)
-                ga[j + z] = g
                 rows.append(g)
         for n in range(unroll // 8):
             left, right = packed(rows[8 * n : 8 * n + 8])
             gpl[it * (unroll // 8) + n] = left
             gpr[it * (unroll // 8) + n] = right
+        send_chunk(it)
+        for w, g in enumerate(rows):
+            j = it * unroll + w
+            t0[j, block_of(2), :] = g
+            for m, s in SHIFTS:
+                t0[j, block_of(m), :] = rolled(g, s, dn)
         return 0
 
     lax.fori_loop(0, H1 // unroll, body, 0)
@@ -398,8 +452,8 @@
 
 
 def kernel(
-    dil, emb_hbm, w_hbm, bias_hbm, cot_hbm, out_hbm, res, ge,
-    emb, w, bias, cot, out, ec, er, a, rl, rr, pl_, pr_, ga, grl, grr, gpl, gpr, x0, x1, s0, t1, s1, t0, wf, wb, gw, gb,
+    dil, emb_hbm, w_hbm, bias_hbm, cot_hbm, out_hbm, res_hbm, ge_hbm,
+    res, ge,    emb, w, bias, cot, out, ec, er, a, rl, rr, pl_, pr_, grl, grr, gpl, gpr, x0, x1, s0, t1, s1, t0, wf, wb, gw, gb,
     pay, terms, wr1, w2, wr2, inbox, shares, win, caps,
     io, esend, erecv, hsend, hrecv, gsend, grecv, sa, ra, sb, rb, sc, rc, st, rt, su, ru, local_sem,
 ):
@@ -458,6 +512,7 @@
     def column(layer):
         return jnp.sum(jnp.where(eye, bias[layer : layer + 1, :], 0.0), axis=1, keepdims=True)
 
+    phase_own_shifts(row0, band0, d1, a, t1)
     for c in ecopies:
         c.wait_recv()
     bounded_blocks(r, o, ec, er)
@@ -466,17 +521,25 @@
     phase_x1(row0, band0, d0, d1, wf[0], column(0), x0, s0, x1, s1, 48)
     for c in hcopies:
         c.wait_recv()
-    phase_shift(row0, band0, d1, 2 * DMAX, a, rl, rr, t1, 4)
-    phase_g1(d1, wb[1], x1, t1, ga, gpl, gpr)
-    gcopies = [
-        remote(gpl, grl, gsend.at[0], grecv.at[0], wrap(r, o - 1)),
-        remote(gpr, grr, gsend.at[1], grecv.at[1], wrap(r, o + 1)),
-    ]
-    for c in gcopies:
-        c.start()
+    phase_rim_shifts(row0, band0, d1, a, t1)
+    phase_patch(row0, band0, d1, 2 * DMAX, H2 // 8, rl, rr, t1, 5)
+
+    def edge_copies(it):
+        part = pl.ds(it * 6, 6)
+        return (
+            remote(gpl.at[part], grl.at[part], gsend.at[it], grecv.at[it], wrap(r, o - 1)),
+            remote(gpr.at[part], grr.at[part], gsend.at[3 + it], grecv.at[3 + it], wrap(r, o + 1)),
+        )
+
+    def send_chunk(it):
+        for c in edge_copies(it):
+            c.start()
+
+    phase_g1(d1, d0, wb[1], x1, t1, t0, gpl, gpr, send_chunk)
+    gcopies = [c for n in range(3) for c in edge_copies(n)]
     phase_gw(lambda i: t1[i + 2 * DMAX, 64:96, :], s1, DMAX, d1, gw, gb)
     third1 = pack_grads(1, gw, gb, pay)
-    phase_gw(lambda i: ga[i + DMAX], s0, 2 * DMAX, d0, gw, gb)
+    phase_gw(lambda i: t0[i + DMAX, 64:96, :], s0, 2 * DMAX, d0, gw, gb)
     third0 = pack_grads(0, gw, gb, pay)
     rest = third0 + pltpu.roll(third1, 64, 1)
     for n in range(16):
@@ -489,7 +552,8 @@
 
     for c in gcopies:
         c.wait_recv()
-    phase_shift(row0, band0, d0, DMAX, ga, grl, grr, t0, 3)
+    phase_patch(row0, band0, d0, DMAX, H1 // 8, grl, grr, t0, 6)
+
     def arrived(dst, sem):
         pltpu.make_async_copy(dst, dst, sem).wait()
 
@@ -499,8 +563,6 @@
             acc = acc + buf[n]
         return acc
 
-    zero = jnp.zeros((CH, TI), f32)
-    sums = phase_g0(d0, wb[0], s0, t0, 0, 64, (zero, zero, zero))
     wr1[me] = pay[me]
     for n in range(1, 16):
         other, _t = peer_a(n)
@@ -511,7 +573,8 @@
     for c in second:
         c.start()
 
-    rsum, lo, hi = phase_g0(d0, wb[0], s0, t0, 64, 128, sums)
+    zero = jnp.zeros((CH, TI), f32)
+    rsum, lo, hi = phase_g0(d0, wb[0], s0, t0, 0, 128, (zero, zero, zero))
     terms[0] = lo
     terms[1] = hi
     low = remote(terms.at[0], inbox.at[0], st.at[0], rt.at[0], wrap(r + o, o))
@@ -561,9 +624,13 @@
     for n in range(1, 8):
         acc = acc + shares[n]
     ge[...] = acc
+    write_ge = pltpu.make_async_copy(ge, ge_hbm, io.at[5])
+    write_ge.start()
     for n in range(1, 16):
         other, _t = peer_a(n)
         arrived(res.at[other], rc.at[other])
+    write_res = pltpu.make_async_copy(res, res_hbm, io.at[6])
+    write_res.start()
     for c in first + second + third + [high] + eall + ecopies + hcopies + gcopies:
         c.wait_send()
 
@@ -571,22 +638,32 @@
     def _():
         low.wait_send()
 
-    write.wait()
-
-
-def finish(section, res, ge, out, gw_out, gb_out, ge_out, held, come, go):
+    for c in (write, write_ge, write_res):
+        c.wait()
+
+
+def finish(section, res, ge, out, gw_out, gb_out, ge_out, held, rv, gv, gwv, gbv, come, go):
     size = CH // 4
     parts = [slice(n * size, n * size + size) for n in range(4)]
     ins = [pltpu.make_async_copy(section.at[p], held.at[p], come.at[n]) for n, p in enumerate(parts)]
     outs = [pltpu.make_async_copy(held.at[p], out.at[p], go.at[n]) for n, p in enumerate(parts)]
-    for c in ins:
+    res_in = pltpu.make_async_copy(res, rv, come.at[4])
+    ge_in = pltpu.make_async_copy(ge, gv, come.at[5])
+    for c in [res_in, ge_in] + ins:
+        c.start()
+    small = [
+        pltpu.make_async_copy(src, dst, go.at[4 + n])
+        for n, (src, dst) in enumerate(((gwv, gw_out), (gbv, gb_out), (gv, ge_out)))
+    ]
+    res_in.wait()
+    unpack_grads(rv, gwv, gbv)
+    ge_in.wait()
+    for c in small:
         c.start()
     for n in range(4):
         ins[n].wait()
         outs[n].start()
-    unpack_grads(res, gw_out, gb_out)
-    ge_out[...] = ge[...]
-    for c in outs:
+    for c in outs + small:
         c.wait()
 
 
@@ -599,13 +676,14 @@
     mem = pltpu.VMEM
     halo = [mem((H2, CH, 128), bf16), mem((20, CH, 128), bf16), mem((20, CH, 128), bf16),
             mem((16, CH, 128), bf16), mem((16, CH, 128), bf16)]
-    edge = [mem((H1, CH, 128), bf16)] + [mem((18, CH, 128), bf16)] * 4
+    edge = [mem((18, CH, 128), bf16)] * 4
     section, res, ge = pl.pallas_call(
         kernel,
         out_shape=[shape((CH, TI, TK), bf16), shape((16, 2, 8, 128), f32), shape((CH, TI), f32)],
         in_specs=[smem, hbm, hbm, hbm, hbm],
-        out_specs=[hbm, vmem, vmem],
+        out_specs=[hbm, hbm, hbm],
         scratch_shapes=[
+            mem((16, 2, 8, 128), f32), mem((CH, TI), f32),
             mem((CH, TI), bf16), mem((2, 9, CH, CH), bf16), mem((2, CH), f32),
             mem((CH, TI, TK), bf16), mem((CH, TI, TK), bf16),
             mem((6, CH, 128), bf16), mem((3, CH, 128), bf16), *halo, *edge,
@@ -618,7 +696,7 @@
             mem((16, 2, 8, 128), f32), mem((2, 8, 128), f32),
             mem((16, 2, 8, 128), f32), mem((2, CH, TI), f32), mem((8, CH, TI), f32),
             mem((H2 + 4 * DMAX, CH, 256), bf16), mem((10, CH, 128), bf16),
-            dma((5,)), dma((6,)), dma((6,)), dma((8,)), dma((8,)), dma((2,)), dma((2,)),
+            dma((7,)), dma((6,)), dma((6,)), dma((8,)), dma((8,)), dma((6,)), dma((6,)),
             dma((16,)), dma((16,)), dma((16,)), dma((16,)), dma((16,)), dma((16,)),
             dma((2,)), dma((2,)), dma((8,)), dma((8,)), dma,
         ],
@@ -628,9 +706,10 @@
     out, gw, gb, ge_out = pl.pallas_call(
         finish,
         out_shape=[shape((CH, TI, TK), bf16), shape((2, 9, CH, CH), f32), shape((2, CH), f32), shape((CH, TI), f32)],
-        in_specs=[hbm, vmem, vmem],
-        out_specs=[hbm, vmem, vmem, vmem],
-        scratch_shapes=[mem((CH, TI, TK), bf16), dma((4,)), dma((4,))],
+        in_specs=[hbm] * 3,
+        out_specs=[hbm] * 4,
+        scratch_shapes=[mem((CH, TI, TK), bf16), mem((16, 2, 8, 128), f32), mem((CH, TI), f32),
+                        mem((2, 9, CH, CH), f32), mem((2, CH), f32), dma((6,)), dma((7,))],
         name="finish",
     )(section, res, ge)
     return out, gw, gb, ge_out

time: 66.6 us -> 63.4 us (0.952)
  Pallas kernels: 65.8 us -> 62.6 us
    pallas_call x1, Pallas kernels: 62.2 us -> 60.4 us  [per_device(): pl.pallas_call(kernel, out_shape=[shape((CH, TI, TK), bf16), shape((16, 2...]
    pallas_call x1, Pallas kernels: 3.61 us -> 2.23 us  [per_device(): pl.pallas_call(finish, out_shape=[shape((CH, TI, TK), bf16), shape((2, 9,...]
where the time goes in v6:
time: 63.4 us; the launch traced here: 63.2 us
  Pallas kernels  62.6 us (99%)
  between operations  0.64 us (1%)
    pallas_call x1, Pallas kernels, per_device(): pl.pallas_call(kernel, out_shape=[shape((CH, TI, TK), bf16), shape((16, 2...  60.4 us
    pallas_call x1, Pallas kernels, per_device(): pl.pallas_call(finish, out_shape=[shape((CH, TI, TK), bf16), shape((2, 9,...  2.23 us

profile of v6, /device:TPU:1, one launch (start us, length us, event | category | flops | bytes accessed | tf_op | source)
XLA Modules:
  0.0 63.2 jit_solution(14052447449833517722)
XLA Ops:
  0.6 60.4 %section.1 = (bf16[32,128,128]{2,1,0:T(8,128)(2,1)}, f32[16,2,8,128]{3,2,1,0:T(8,128)}, f32[32,128]{1,0:T(8,128)}) custom-call(s32[2]{0:T(128)} %dil.1, bf16[32,128]{1,0:T(8,128)(2,1)} %emb_hbm.1, bf16[2,9,32,32]{3,2,1,0:T(8,128)(2,1)} %w_hbm.1, f32[2,32]{1,0:T(2,128)} %bias_hbm.1, bf16[32,128,128]{2,1,0:T(8,128)(2,1)} %cot_hbm.1), custom_call_target="tpu_custom_call" | custom-call | tf_op jit(solution)/shard_map/section/pallas_call | solution.py:680
  61.0 2.2 %finish.1 = (bf16[32,128,128]{2,1,0:T(8,128)(2,1)}, f32[2,9,32,32]{3,2,1,0:T(8,128)}, f32[2,32]{1,0:T(2,128)}, f32[32,128]{1,0:T(8,128)}) custom-call(bf16[32,128,128]{2,1,0:T(8,128)(2,1)} %get-tuple-element.7.section, f32[16,2,8,128]{3,2,1,0:T(8,128)} %get-tuple-element.8.res, f32[32,128]{1,0:T(8,128)} %get-tuple-element.9.ge), custom_call_target="tpu_custom_call" | custom-call | tf_op jit(solution)/shard_map/finish/pallas_call | solution.py:706

commit v7 on v6

--- a/solution.py
+++ b/solution.py
@@ -91,12 +91,16 @@
         er[n] = jnp.where((ec_row >= 0) & (ec_row < NBINS // TI), er[n], LOW)
 
 
+def rim_lane():
+    t = lax.rem(lanes(), 32)
+    return jnp.where(t < 16, t - 16, t + 112)
+
+
 def lane_caps(band0, d, caps):
-    p = lanes()
     for n, s in enumerate((-2, -1, 0, 1, 2)):
-        for half in range(2):
-            k = band0 + s * d + (jnp.where(p < 64, p + 128, p - 128) if half else p)
-            caps[2 * n + half] = jnp.where((k >= 0) & (k < KBAND), 3e38, 0.0).astype(bf16)
+        for rim in range(2):
+            k = band0 + s * d + (rim_lane() if rim else lanes())
+            caps[2 * n + rim] = jnp.where((k >= 0) & (k < KBAND), 3e38, 0.0).astype(bf16)
 
 
 def phase_windows(ec, win, unroll=32):
@@ -121,7 +125,26 @@
     lax.fori_loop(0, (H2 + 4 * DMAX) // unroll, body, 0)
 
 
-def phase_x0(d, er, win, caps, x0, s0, unroll=16):
+def four_groups(rows):
+    p = lanes()
+    low = jnp.where(p < 32, rows[0], rows[1])
+    high = jnp.where(p < 96, rows[2], rows[3])
+    return jnp.where(p < 64, low, high)
+
+
+def phase_rim_windows(win, rwin, unroll=12):
+    def body(it, _):
+        for w in range(unroll):
+            n = it * unroll + w
+            rwin[n] = four_groups(
+                [pltpu.roll(win[36 * q + n, :, 128:256], (32 * q + 16) % 128, 1) for q in range(4)]
+            )
+        return 0
+
+    lax.fori_loop(0, 84 // unroll, body, 0)
+
+
+def phase_x0(d, er, win, caps, x0, s0, owns, unroll=16):
     def body(it, _):
         i0 = it * unroll - 2 * DMAX
         q = lax.div(i0 + 128, 128) - 1
@@ -129,38 +152,78 @@
         for w in range(unroll):
             j = it * unroll + w
             own = jnp.broadcast_to(block[:, w : w + 1], (CH, 128))
+            owns[j] = own
             for n, s in enumerate((-2, -1, 0, 1, 2)):
-                for half in range(2):
-                    at = slice(128 * half, 128 * half + 128)
-                    v = own + win[j + 2 * DMAX + s * d, :, at]
-                    if s == 0:
-                        x0[j, :, at] = v
-                    s0[j, CH * n : CH * n + CH, at] = jnp.minimum(jnp.maximum(v, 0), caps[2 * n + half])
+                v = own + win[j + 2 * DMAX + s * d, :, 0:128]
+                if s == 0:
+                    x0[j] = v
+                s0[j, CH * n : CH * n + CH, :] = jnp.minimum(jnp.maximum(v, 0), caps[2 * n])
         return 0
 
     lax.fori_loop(0, H2 // unroll, body, 0)
 
 
-def phase_x1(row0, band0, d, dn, wf, bias, x0, s0, x1, s1, unroll=4):
-    amounts, insides = shift_tables(dn)
-    bias = jnp.broadcast_to(bias, (CH, 128))
-
+def phase_rim_x0(d, rwin, owns, caps, rx0, rs0, unroll=13):
     def body(it, _):
         for w in range(unroll):
             j = it * unroll + w
+            own = four_groups([owns[36 * q + j] for q in range(4)])
+            for n, s in enumerate((-2, -1, 0, 1, 2)):
+                v = own + rwin[j + 2 * DMAX + s * d]
+                if s == 0:
+                    rx0[j] = v
+                rs0[j, CH * n : CH * n + CH, :] = jnp.minimum(jnp.maximum(v, 0), caps[2 * n + 1])
+        return 0
+
+    lax.fori_loop(0, 52 // unroll, body, 0)
+
+
+def phase_rim_x1(row0, band0, d, wf, bias, rx0, rs0, rx1, unroll=36):
+    bias = jnp.broadcast_to(bias, (CH, 128))
+    k = band0 + rim_lane()
+    across = (k >= 0) & (k < KBAND)
+
+    def body(it, _):
+        for w in range(0, unroll, 2):
+            j = it * unroll + w
+            x = jnp.concatenate([taps(rs0, j + DMAX, d, 0, 128), taps(rs0, j + DMAX + 1, d, 0, 128)], axis=1)
+            conv = jnp.dot(wf, x, preferred_element_type=f32)
+            for z in range(2):
+                row = row0 + 36 * lax.div(lanes(), 32) + (j + z - DMAX)
+                v = rx0[j + z + DMAX].astype(f32) + conv[:, 128 * z : 128 * z + 128] + bias
+                live = across & (row >= 0) & (k < NBINS - row)
+                rx1[j + z] = jnp.where(live, jnp.maximum(v, 0.0), 0.0).astype(bf16)
+        return 0
+
+    lax.fori_loop(0, 36 // unroll, body, 0)
+
+
+def phase_x1(row0, band0, d, dn, wf, bias, x0, s0, rx1, x1, s1):
+    insides = inside_masks(dn)
+    bias = jnp.broadcast_to(bias, (CH, 128))
+    lane = lanes()
+
+    def body(it, _):
+        for w in range(0, 36, 2):
+            j = it * 36 + w
             jj = j + DMAX
-            conv = jnp.dot(wf, taps(s0, jj, d), preferred_element_type=f32)
-            ma, mb = row_masks(row0, band0, j - DMAX)
-            a = x0[jj, :, 0:128].astype(f32) + conv[:, 0:128] + bias
-            b = x0[jj, :, 128:256].astype(f32) + conv[:, 128:256] + bias
-            a = jnp.where(ma, a, 0.0).astype(bf16)
-            b = jnp.where(mb, b, 0.0).astype(bf16)
-            x1[j, :, 0:128] = a
-            x1[j, :, 128:256] = b
-            store_shifts(s1, j, jnp.maximum(a, 0), jnp.maximum(b, 0), amounts, insides, False)
-        return 0
-
-    lax.fori_loop(0, H1 // unroll, body, 0)
+            x = jnp.concatenate([taps(s0, jj, d, 0, 128), taps(s0, jj + 1, d, 0, 128)], axis=1)
+            conv = jnp.dot(wf, x, preferred_element_type=f32)
+            for z in range(2):
+                row = row0 + j + z - DMAX
+                live = (row >= 0) & (band0 + lane < NBINS - row)
+                a = x0[jj + z].astype(f32) + conv[:, 128 * z : 128 * z + 128] + bias
+                a = jnp.where(live, a, 0.0).astype(bf16)
+                x1[j + z] = a
+                a = jnp.maximum(a, 0)
+                s1[j + z, block_of(2), :] = a
+                rim = rx1[w + z]
+                for n, (m, s) in enumerate(SHIFTS):
+                    side = pltpu.roll(rim, lax.rem(384 + 112 - 32 * it - s * dn, 128), 1)
+                    s1[j + z, block_of(m), :] = jnp.where(insides[n], rolled(a, s, dn), side)
+        return 0
+
+    lax.fori_loop(0, 4, body, 0)
 
 
 def phase_x2(row0, band0, d, wf, bias, x1, s1, out, unroll=16):
@@ -175,7 +238,7 @@
             conv = jnp.dot(wf, x, preferred_element_type=f32)
             for z in range(2):
                 ma, _mb = row_masks(row0, band0, i + z)
-                a = x1[j + z, :, 0:128].astype(f32) + conv[:, 128 * z : 128 * z + 128] + bias
+                a = x1[j + z].astype(f32) + conv[:, 128 * z : 128 * z + 128] + bias
                 rows.append(jnp.where(ma, a, 0.0).astype(bf16))
         out[:, pl.ds(pl.multiple_of(it * unroll, unroll), unroll), :] = jnp.swapaxes(jnp.stack(rows), 0, 1)
         return 0
@@ -304,7 +367,7 @@
             q = jnp.dot(wb, x, preferred_element_type=f32)
             for z in range(2):
                 h = t1[j + DMAX + z, 64:96, :].astype(f32)
-                gate = x1[j + z, :, 0:128].astype(f32) > 0
+                gate = x1[j + z].astype(f32) > 0
                 g = (h + jnp.where(gate, q[:, 128 * z : 128 * z + 128], 0.0)).astype(bf16)
                 rows.append(g)
         for n in range(unroll // 8):
@@ -454,7 +517,7 @@
 def kernel(
     dil, emb_hbm, w_hbm, bias_hbm, cot_hbm, out_hbm, res_hbm, ge_hbm,
     res, ge,    emb, w, bias, cot, out, ec, er, a, rl, rr, pl_, pr_, grl, grr, gpl, gpr, x0, x1, s0, t1, s1, t0, wf, wb, gw, gb,
-    pay, terms, wr1, w2, wr2, inbox, shares, win, caps,
+    pay, terms, wr1, w2, wr2, inbox, shares, win, caps, rwin, owns, rx0, rs0, rx1,
     io, esend, erecv, hsend, hrecv, gsend, grecv, sa, ra, sb, rb, sc, rc, st, rt, su, ru, local_sem,
 ):
     r, o = lax.axis_index("diag"), lax.axis_index("off")
@@ -517,8 +580,11 @@
         c.wait_recv()
     bounded_blocks(r, o, ec, er)
     phase_windows(ec, win)
-    phase_x0(d0, er, win, caps, x0, s0)
-    phase_x1(row0, band0, d0, d1, wf[0], column(0), x0, s0, x1, s1, 48)
+    phase_rim_windows(win, rwin)
+    phase_x0(d0, er, win, caps, x0, s0, owns)
+    phase_rim_x0(d0, rwin, owns, caps, rx0, rs0)
+    phase_rim_x1(row0, band0, d0, wf[0], column(0), rx0, rs0, rx1)
+    phase_x1(row0, band0, d0, d1, wf[0], column(0), x0, s0, rx1, x1, s1)
     for c in hcopies:
         c.wait_recv()
     phase_rim_shifts(row0, band0, d1, a, t1)
@@ -563,6 +629,8 @@
             acc = acc + buf[n]
         return acc
 
+    zero = jnp.zeros((CH, TI), f32)
+    sums = phase_g0(d0, wb[0], s0, t0, 0, 64, (zero, zero, zero))
     wr1[me] = pay[me]
     for n in range(1, 16):
         other, _t = peer_a(n)
@@ -573,8 +641,7 @@
     for c in second:
         c.start()
 
-    zero = jnp.zeros((CH, TI), f32)
-    rsum, lo, hi = phase_g0(d0, wb[0], s0, t0, 0, 128, (zero, zero, zero))
+    rsum, lo, hi = phase_g0(d0, wb[0], s0, t0, 64, 128, sums)
     terms[0] = lo
     terms[1] = hi
     low = remote(terms.at[0], inbox.at[0], st.at[0], rt.at[0], wrap(r + o, o))
@@ -687,8 +754,8 @@
             mem((CH, TI), bf16), mem((2, 9, CH, CH), bf16), mem((2, CH), f32),
             mem((CH, TI, TK), bf16), mem((CH, TI, TK), bf16),
             mem((6, CH, 128), bf16), mem((3, CH, 128), bf16), *halo, *edge,
-            mem((H2, CH, 256), bf16), mem((H1, CH, 256), bf16),
-            mem((H2, 5 * CH, 256), bf16), mem((H2, 5 * CH, 128), bf16),
+            mem((H2, CH, 128), bf16), mem((H1, CH, 128), bf16),
+            mem((H2, 5 * CH, 128), bf16), mem((H2, 5 * CH, 128), bf16),
             mem((H1, 5 * CH, 128), bf16), mem((H1, 5 * CH, 128), bf16),
             mem((2, CH, 9 * CH), bf16), mem((2, CH, 9 * CH), bf16),
             mem((CH, 9 * CH), f32), mem((CH, 128), f32),
@@ -696,6 +763,8 @@
             mem((16, 2, 8, 128), f32), mem((2, 8, 128), f32),
             mem((16, 2, 8, 128), f32), mem((2, CH, TI), f32), mem((8, CH, TI), f32),
             mem((H2 + 4 * DMAX, CH, 256), bf16), mem((10, CH, 128), bf16),
+            mem((84, CH, 128), bf16), mem((H2, CH, 128), bf16), mem((52, CH, 128), bf16),
+            mem((52, 5 * CH, 128), bf16), mem((36, CH, 128), bf16),
             dma((7,)), dma((6,)), dma((6,)), dma((8,)), dma((8,)), dma((6,)), dma((6,)),
             dma((16,)), dma((16,)), dma((16,)), dma((16,)), dma((16,)), dma((16,)),
             dma((2,)), dma((2,)), dma((8,)), dma((8,)), dma,

time: 63.4 us -> 62.4 us (0.984)
  Pallas kernels: 62.6 us -> 61.6 us
    pallas_call x1, Pallas kernels: 60.4 us -> 59.4 us  [per_device(): pl.pallas_call(kernel, out_shape=[shape((CH, TI, TK), bf16), shape((16, 2...]
where the time goes in v7:
time: 62.4 us; the launch traced here: 62.3 us
  Pallas kernels  61.6 us (99%)
  between operations  0.64 us (1%)
    pallas_call x1, Pallas kernels, per_device(): pl.pallas_call(kernel, out_shape=[shape((CH, TI, TK), bf16), shape((16, 2...  59.4 us
    pallas_call x1, Pallas kernels, per_device(): pl.pallas_call(finish, out_shape=[shape((CH, TI, TK), bf16), shape((2, 9,...  2.23 us

profile of v7, /device:TPU:1, one launch (start us, length us, event | category | flops | bytes accessed | tf_op | source)
XLA Modules:
  0.0 62.3 jit_solution(389657991618768595)
XLA Ops:
  0.6 59.4 %section.1 = (bf16[32,128,128]{2,1,0:T(8,128)(2,1)}, f32[16,2,8,128]{3,2,1,0:T(8,128)}, f32[32,128]{1,0:T(8,128)}) custom-call(s32[2]{0:T(128)} %dil.1, bf16[32,128]{1,0:T(8,128)(2,1)} %emb_hbm.1, bf16[2,9,32,32]{3,2,1,0:T(8,128)(2,1)} %w_hbm.1, f32[2,32]{1,0:T(2,128)} %bias_hbm.1, bf16[32,128,128]{2,1,0:T(8,128)(2,1)} %cot_hbm.1), custom_call_target="tpu_custom_call" | custom-call | tf_op jit(solution)/shard_map/section/pallas_call | solution.py:747
  60.0 2.2 %finish.1 = (bf16[32,128,128]{2,1,0:T(8,128)(2,1)}, f32[2,9,32,32]{3,2,1,0:T(8,128)}, f32[2,32]{1,0:T(2,128)}, f32[32,128]{1,0:T(8,128)}) custom-call(bf16[32,128,128]{2,1,0:T(8,128)(2,1)} %get-tuple-element.7.section, f32[16,2,8,128]{3,2,1,0:T(8,128)} %get-tuple-element.8.res, f32[32,128]{1,0:T(8,128)} %get-tuple-element.9.ge), custom_call_target="tpu_custom_call" | custom-call | tf_op jit(solution)/shard_map/finish/pallas_call | solution.py:775

commit v8 on v7

--- a/solution.py
+++ b/solution.py
@@ -585,9 +585,13 @@
     phase_rim_x0(d0, rwin, owns, caps, rx0, rs0)
     phase_rim_x1(row0, band0, d0, wf[0], column(0), rx0, rs0, rx1)
     phase_x1(row0, band0, d0, d1, wf[0], column(0), x0, s0, rx1, x1, s1)
-    for c in hcopies:
+    phase_gw(lambda i: t1[i + 2 * DMAX, 64:96, :], s1, DMAX, d1, gw, gb)
+    third1 = pack_grads(1, gw, gb, pay)
+    for c in hcopies[2:4]:
         c.wait_recv()
     phase_rim_shifts(row0, band0, d1, a, t1)
+    for c in hcopies[:2] + hcopies[4:]:
+        c.wait_recv()
     phase_patch(row0, band0, d1, 2 * DMAX, H2 // 8, rl, rr, t1, 5)
 
     def edge_copies(it):
@@ -603,8 +607,6 @@
 
     phase_g1(d1, d0, wb[1], x1, t1, t0, gpl, gpr, send_chunk)
     gcopies = [c for n in range(3) for c in edge_copies(n)]
-    phase_gw(lambda i: t1[i + 2 * DMAX, 64:96, :], s1, DMAX, d1, gw, gb)
-    third1 = pack_grads(1, gw, gb, pay)
     phase_gw(lambda i: t0[i + DMAX, 64:96, :], s0, 2 * DMAX, d0, gw, gb)
     third0 = pack_grads(0, gw, gb, pay)
     rest = third0 + pltpu.roll(third1, 64, 1)
@@ -615,6 +617,10 @@
              for n in range(1, 16) for other, target in [peer_a(n)]]
     for c in first:
         c.start()
+
+    phase_x2(row0, band0, d1, wf[1], column(1), x1, s1, out, 64)
+    write = pltpu.make_async_copy(out, out_hbm, io.at[4])
+    write.start()
 
     for c in gcopies:
         c.wait_recv()
@@ -657,9 +663,6 @@
     def _():
         local.start()
 
-    phase_x2(row0, band0, d1, wf[1], column(1), x1, s1, out, 64)
-    write = pltpu.make_async_copy(out, out_hbm, io.at[4])
-    write.start()
 
     @pl.when(o > 0)
     def _():

time: 62.4 us -> 63.5 us (1.018)
  Pallas kernels: 61.6 us -> 62.7 us
    pallas_call x1, Pallas kernels: 59.4 us -> 60.5 us  [per_device(): pl.pallas_call(kernel, out_shape=[shape((CH, TI, TK), bf16), shape((16, 2...]
where the time goes in v8:
time: 63.5 us; the launch traced here: 63.4 us
  Pallas kernels  62.7 us (99%)
  between operations  0.64 us (1%)
    pallas_call x1, Pallas kernels, per_device(): pl.pallas_call(kernel, out_shape=[shape((CH, TI, TK), bf16), shape((16, 2...  60.5 us
    pallas_call x1, Pallas kernels, per_device(): pl.pallas_call(finish, out_shape=[shape((CH, TI, TK), bf16), shape((2, 9,...  2.23 us

profile of v8, /device:TPU:1, one launch (start us, length us, event | category | flops | bytes accessed | tf_op | source)
XLA Modules:
  0.0 63.4 jit_solution(6842035149208787668)
XLA Ops:
  0.6 60.5 %section.1 = (bf16[32,128,128]{2,1,0:T(8,128)(2,1)}, f32[16,2,8,128]{3,2,1,0:T(8,128)}, f32[32,128]{1,0:T(8,128)}) custom-call(s32[2]{0:T(128)} %dil.1, bf16[32,128]{1,0:T(8,128)(2,1)} %emb_hbm.1, bf16[2,9,32,32]{3,2,1,0:T(8,128)(2,1)} %w_hbm.1, f32[2,32]{1,0:T(2,128)} %bias_hbm.1, bf16[32,128,128]{2,1,0:T(8,128)(2,1)} %cot_hbm.1), custom_call_target="tpu_custom_call" | custom-call | tf_op jit(solution)/shard_map/section/pallas_call | solution.py:750
  61.1 2.2 %finish.1 = (bf16[32,128,128]{2,1,0:T(8,128)(2,1)}, f32[2,9,32,32]{3,2,1,0:T(8,128)}, f32[2,32]{1,0:T(2,128)}, f32[32,128]{1,0:T(8,128)}) custom-call(bf16[32,128,128]{2,1,0:T(8,128)(2,1)} %get-tuple-element.7.section, f32[16,2,8,128]{3,2,1,0:T(8,128)} %get-tuple-element.8.res, f32[32,128]{1,0:T(8,128)} %get-tuple-element.9.ge), custom_call_target="tpu_custom_call" | custom-call | tf_op jit(solution)/shard_map/finish/pallas_call | solution.py:778

commit v9 on v7

--- a/solution.py
+++ b/solution.py
@@ -585,9 +585,11 @@
     phase_rim_x0(d0, rwin, owns, caps, rx0, rs0)
     phase_rim_x1(row0, band0, d0, wf[0], column(0), rx0, rs0, rx1)
     phase_x1(row0, band0, d0, d1, wf[0], column(0), x0, s0, rx1, x1, s1)
-    for c in hcopies:
+    for c in hcopies[2:4]:
         c.wait_recv()
     phase_rim_shifts(row0, band0, d1, a, t1)
+    for c in hcopies[:2] + hcopies[4:]:
+        c.wait_recv()
     phase_patch(row0, band0, d1, 2 * DMAX, H2 // 8, rl, rr, t1, 5)
 
     def edge_copies(it):
@@ -684,6 +686,13 @@
              for n in range(1, 16) for other, target in [peer_a(n)]]
     for c in third:
         c.start()
+    for c in ecopies + hcopies + gcopies + first + second + [high]:
+        c.wait_send()
+
+    @pl.when(o > 0)
+    def _():
+        low.wait_send()
+
     for n in range(1, 8):
         oo = lax.rem(o + n, 8)
         arrived(shares.at[oo], ru.at[oo])
@@ -698,12 +707,8 @@
         arrived(res.at[other], rc.at[other])
     write_res = pltpu.make_async_copy(res, res_hbm, io.at[6])
     write_res.start()
-    for c in first + second + third + [high] + eall + ecopies + hcopies + gcopies:
+    for c in third + eall:
         c.wait_send()
-
-    @pl.when(o > 0)
-    def _():
-        low.wait_send()
 
     for c in (write, write_ge, write_res):
         c.wait()

time: 62.4 us -> 62.4 us (level)
  no operation moved by 1% of the time
where the time goes in v9:
time: 62.4 us; the launch traced here: 62.3 us
  Pallas kernels  61.6 us (99%)
  between operations  0.64 us (1%)
    pallas_call x1, Pallas kernels, per_device(): pl.pallas_call(kernel, out_shape=[shape((CH, TI, TK), bf16), shape((16, 2...  59.4 us
    pallas_call x1, Pallas kernels, per_device(): pl.pallas_call(finish, out_shape=[shape((CH, TI, TK), bf16), shape((2, 9,...  2.23 us

profile of v9, /device:TPU:1, one launch (start us, length us, event | category | flops | bytes accessed | tf_op | source)
XLA Modules:
  0.0 62.3 jit_solution(10334718652831351994)
XLA Ops:
  0.6 59.4 %section.1 = (bf16[32,128,128]{2,1,0:T(8,128)(2,1)}, f32[16,2,8,128]{3,2,1,0:T(8,128)}, f32[32,128]{1,0:T(8,128)}) custom-call(s32[2]{0:T(128)} %dil.1, bf16[32,128]{1,0:T(8,128)(2,1)} %emb_hbm.1, bf16[2,9,32,32]{3,2,1,0:T(8,128)(2,1)} %w_hbm.1, f32[2,32]{1,0:T(2,128)} %bias_hbm.1, bf16[32,128,128]{2,1,0:T(8,128)(2,1)} %cot_hbm.1), custom_call_target="tpu_custom_call" | custom-call | tf_op jit(solution)/shard_map/section/pallas_call | solution.py:752
  60.0 2.2 %finish.1 = (bf16[32,128,128]{2,1,0:T(8,128)(2,1)}, f32[2,9,32,32]{3,2,1,0:T(8,128)}, f32[2,32]{1,0:T(2,128)}, f32[32,128]{1,0:T(8,128)}) custom-call(bf16[32,128,128]{2,1,0:T(8,128)(2,1)} %get-tuple-element.7.section, f32[16,2,8,128]{3,2,1,0:T(8,128)} %get-tuple-element.8.res, f32[32,128]{1,0:T(8,128)} %get-tuple-element.9.ge), custom_call_target="tpu_custom_call" | custom-call | tf_op jit(solution)/shard_map/finish/pallas_call | solution.py:780
